TPU v7x, 768 devices: a whole 4x8x12 slice. The times are simulated.
768 devices in a mesh: rows: 64 (over y, z_hi, core), cols: 12 (over x, z_lo).
Axes of the slice: x: 4, y: 8, z: 12 (z_hi: 4, z_lo: 3; z = z_hi * 3 + z_lo), core: 2. Of those that a mesh axis runs over, the one named last changes fastest.
Arguments:
- wind_row: float32 [64, 1024, 1536], P(None, 'rows', 'cols'), may hold values from -6 to 6
- wind_col: float32 [64, 1024, 1536], P(None, 'rows', 'cols'), may hold values from -6 to 6
- wind_up: float32 [64, 1024, 1536], P(None, 'rows', 'cols'), may hold values from -6 to 6
- pressure: float32 [64, 1024, 1536], P(None, 'rows', 'cols'), may hold values from -6 to 6
- courant: bfloat16 [64, 1024, 1536], P(None, 'rows', 'cols'), may hold values from 0.5 to 1
- stiffness: bfloat16 [64, 1024, 1536], P(None, 'rows', 'cols'), may hold values from 0.3 to 6
Outputs:
- out_row: float32 [64, 1024, 1536], P(None, 'rows', 'cols')
- out_col: float32 [64, 1024, 1536], P(None, 'rows', 'cols')
- out_up: float32 [64, 1024, 1536], P(None, 'rows', 'cols')
- out_pressure: float32 [64, 1024, 1536], P(None, 'rows', 'cols')
All inputs are finite; a program needn't handle non-finite values.
Results may differ from a plain program's by a relative error of at most 0.0003.
Values sent between devices are 32-bit elements; how exact they have to be, the bound alone decides.
A program may use at most 64 MiB of HBM per device.

v0:
```python
import functools

import jax
import jax.numpy as jnp
from jax import lax
from jax.experimental import pallas as pl
from jax.experimental.pallas import tpu as pltpu
from jax.sharding import PartitionSpec as P

LEVELS = 64
HALF = LEVELS // 2
ROWS = 16
LANES = 128
BASE = 8
CHUNK = 4
STEPS = HALF // CHUNK
F32 = jnp.float32


def turn(x, shift):
    return pltpu.roll(x, shift % LANES if isinstance(shift, int) else shift, x.ndim - 1)


def kernel(
    u_in, v_in, w_in, p_in, c_in, s_in,
    u_out, v_out, w_out, p_out,
    PR, UR, V, W, C16, S16, H, S, E, G, Y, M,
    RS1, RR1, RS2, RR2, CS1, CR1, CS2, CR2, OWN, EDGE, NEXT,
    in_sems, out_sems, send_sems, recv_sems,
):
    row, col = lax.axis_index("rows"), lax.axis_index("cols")
    nrow, ncol = lax.axis_size("rows"), lax.axis_size("cols")
    up, down = lax.rem(row + 1, nrow), lax.rem(row + nrow - 1, nrow)
    right, left = lax.rem(col + 1, ncol), lax.rem(col + ncol - 1, ncol)
    targets = [(up, col), (down, col), (row, right), (row, left)]

    own_rows = slice(BASE, BASE + ROWS)
    loads = [
        pltpu.make_async_copy(p_in, PR.at[pl.ds(0, LEVELS), pl.ds(BASE, ROWS), :], in_sems.at[0]),
        pltpu.make_async_copy(c_in, C16, in_sems.at[1]),
        pltpu.make_async_copy(u_in, UR.at[:, pl.ds(BASE, ROWS), :], in_sems.at[2]),
        pltpu.make_async_copy(v_in, V, in_sems.at[3]),
        pltpu.make_async_copy(s_in, S16, in_sems.at[4]),
        pltpu.make_async_copy(w_in, W.at[pl.ds(1, LEVELS)], in_sems.at[5]),
    ]
    for load in loads:
        load.start()

    barrier = pltpu.get_barrier_semaphore()
    for target in targets:
        pl.semaphore_signal(barrier, inc=1, device_id=target, device_id_type=pl.DeviceIdType.MESH)

    zero = jnp.zeros((ROWS, LANES), F32)
    W[0] = zero
    PR[LEVELS, own_rows, :] = zero

    lane = lax.broadcasted_iota(jnp.int32, (ROWS, LANES), 1)
    slot = lax.rem(lane, 4)
    group = lax.div(lane, 4)
    first_lane, last_lane = lane == 0, lane == LANES - 1
    ends = first_lane | last_lane

    for load in loads[:3]:
        load.wait()

    def halve(i, carry):
        k = pl.ds(i * 8, 8)
        H[k] = C16[k].astype(F32) * 0.5
        return carry

    lax.fori_loop(0, LEVELS // 8, halve, 0)

    p_lo, p_lo2 = PR[0:LEVELS, BASE, :], PR[0:LEVELS, BASE + 1, :]
    p_hi, p_hi2 = PR[0:LEVELS, BASE + ROWS - 1, :], PR[0:LEVELS, BASE + ROWS - 2, :]
    h_lo, h_hi = H[:, 0, :], H[:, ROWS - 1, :]
    RS1[0, 0] = p_hi
    RS1[0, 1] = UR[:, BASE + ROWS - 1, :] + h_hi * p_hi2
    RS1[0, 2] = h_hi
    RS1[1, 0] = p_lo
    RS1[1, 1] = UR[:, BASE, :] - h_lo * p_lo2
    RS1[1, 2] = h_lo

    pl.semaphore_wait(barrier, 4)

    def send(source, landing, which, direction):
        copy = pltpu.make_async_remote_copy(
            src_ref=source,
            dst_ref=landing,
            send_sem=send_sems.at[which, direction],
            recv_sem=recv_sems.at[which, direction],
            device_id=targets[direction],
            device_id_type=pl.DeviceIdType.MESH,
        )
        copy.start()
        return copy

    first = [send(RS1.at[0], RR1.at[0], 0, 0), send(RS1.at[1], RR1.at[1], 0, 1)]

    loads[3].wait()

    def pack_first(i, carry):
        out = list(carry)
        for half in range(2):
            for j in range(CHUNK):
                kappa = i * CHUNK + j
                k = half * HALF + kappa
                mask = group == kappa
                pp = turn(PR[k, own_rows, :], lax.rem(4 * kappa + 2, LANES))
                vh = jnp.where(ends, V[k], turn(H[k], 2))
                vh = turn(vh, lax.rem(4 * kappa + 1, LANES))
                out[half] = jnp.where(mask, pp, out[half])
                out[2 + half] = jnp.where(mask, vh, out[2 + half])
        return tuple(out)

    packed = lax.fori_loop(0, STEPS, pack_first, (zero, zero, zero, zero))
    for g in range(2):
        pp, vh = packed[g], packed[2 + g]
        OWN[g] = pp
        CS1[0, g] = jnp.where(slot < 2, pp, jnp.where(slot == 2, vh, turn(vh, 3)))
        CS1[1, g] = jnp.where(slot == 0, turn(vh, -3), jnp.where(slot == 1, vh, pp))
    first += [send(CS1.at[0], CR1.at[0], 0, 2), send(CS1.at[1], CR1.at[1], 0, 3)]

    loads[4].wait()

    def factor(i, carry):
        above, below = carry
        for j in range(CHUNK):
            k = i * CHUNK + j
            stiff = S16[k].astype(F32)
            S[k] = stiff
            weight = stiff * stiff
            inverse = 1.0 / (1.0 + 2.0 * weight - weight * above)
            above = weight * inverse
            E[k] = inverse
            G[k] = above
            k = LEVELS - 1 - i * CHUNK - j
            stiff = S16[k].astype(F32)
            S[k] = stiff
            weight = stiff * stiff
            inverse = 1.0 / (1.0 + 2.0 * weight - weight * below)
            below = weight * inverse
            E[k] = inverse
            G[k] = below
        return above, below

    above, below = lax.fori_loop(0, STEPS, factor, (zero, zero))
    M[...] = 1.0 / (1.0 - above * below)
    loads[5].wait()

    at_left, at_right = col == 0, col == ncol - 1
    walled = (((slot == 1) | (slot == 3)) & at_left) | (((slot == 0) | (slot == 2)) & at_right)

    def edges(g, from_left, from_right):
        own = OWN[g]
        taken = from_left * (own - turn(from_left, 2))
        v_left = from_left - turn(taken, 1)
        taken = from_right * (turn(from_right, -3) - turn(own, -1))
        v_right = from_right - turn(taken, 1)
        edge = jnp.where(
            slot == 0,
            turn(from_right, -2),
            jnp.where(slot == 1, from_left, jnp.where(slot == 2, turn(v_right, 1), v_left)),
        )
        EDGE[g] = jnp.where(walled, 0.0, edge)
        NEXT[0, g] = jnp.where(slot == 3, v_left, from_left)
        NEXT[1, g] = jnp.where(slot == 1, v_right, from_right)

    def sweep_in(i, carry):
        chain = list(carry)
        for half in range(2):
            k0 = i * CHUNK if half == 0 else LEVELS - CHUNK - i * CHUNK
            ks = pl.ds(k0, CHUNK)
            here = PR[ks, own_rows, :]
            h = H[ks]
            u1 = UR[ks, own_rows, :] - h * (
                PR[ks, BASE + 1 : BASE + ROWS + 1, :] - PR[ks, BASE - 1 : BASE + ROWS - 1, :]
            )
            UR[ks, own_rows, :] = u1
            below_edge, above_edge, v_edge = [], [], []
            for j in range(CHUNK):
                kappa = k0 + j - half * HALF
                edge = EDGE[half]
                ep = turn(edge, lax.rem(LANES + 127 - 4 * kappa, LANES))
                ev = turn(edge, lax.rem(LANES + 125 - 4 * kappa, LANES))
                k = k0 + j
                p_here = here[j]
                ahead = jnp.where(last_lane, ep, turn(p_here, -1))
                behind = jnp.where(first_lane, ep, turn(p_here, 1))
                v1 = V[k] - h[j] * (ahead - behind)
                V[k] = v1
                ahead = jnp.where(last_lane, ev, turn(v1, -1))
                behind = jnp.where(first_lane, ev, turn(v1, 1))
                v_edge.append(ahead - behind)
            du = UR[ks, BASE + 1 : BASE + ROWS + 1, :] - UR[ks, BASE - 1 : BASE + ROWS - 1, :]
            for j in range(CHUNK) if half == 0 else range(CHUNK - 1, -1, -1):
                k = k0 + j
                source = here[j] - h[j] * (du[j] + v_edge[j]) - S[k] * (W[k + 1] - W[k])
                chain[half] = E[k] * source + G[k] * chain[half]
                Y[k] = chain[half]
        return tuple(chain)

    def sweep_out(step, carry):
        q_top, q_bot, pack_top, pack_bot = carry
        for j in range(CHUNK):
            kappa = HALF - 1 - step * CHUNK - j
            q_top = Y[kappa] + G[kappa] * q_top
            PR[kappa, own_rows, :] = q_top
            pack_top = jnp.where(group == kappa, turn(q_top, lax.rem(4 * kappa + 2, LANES)), pack_top)
            kappa = step * CHUNK + j
            k = HALF + kappa
            q_bot = Y[k] + G[k] * q_bot
            PR[k, own_rows, :] = q_bot
            pack_bot = jnp.where(group == kappa, turn(q_bot, lax.rem(4 * kappa + 2, LANES)), pack_bot)
        return q_top, q_bot, pack_top, pack_bot

    def solve():
        y_top, y_bot = lax.fori_loop(0, STEPS, sweep_in, (zero, zero))
        q_bot = (y_bot + G[HALF] * y_top) * M[...]
        q_top = y_top + G[HALF - 1] * q_bot
        return lax.fori_loop(0, STEPS, sweep_out, (q_bot, q_top, zero, zero))

    def lift(i, carry):
        k0 = i * CHUNK
        W[pl.ds(k0 + 1, CHUNK)] = W[pl.ds(k0 + 1, CHUNK)] - S[pl.ds(k0, CHUNK)] * (
            PR[pl.ds(k0 + 1, CHUNK), own_rows, :] - PR[pl.ds(k0, CHUNK), own_rows, :]
        )
        return carry

    for copy in first:
        copy.wait_recv()

    PR[0:LEVELS, BASE - 1, :] = RR1[0, 0]
    PR[0:LEVELS, BASE + ROWS, :] = RR1[1, 0]
    UR[:, BASE - 1, :] = RR1[0, 1] - RR1[0, 2] * PR[0:LEVELS, BASE, :]
    UR[:, BASE + ROWS, :] = RR1[1, 1] + RR1[1, 2] * PR[0:LEVELS, BASE + ROWS - 1, :]
    for g in range(2):
        edges(g, CR1[0, g], CR1[1, g])

    unused, unused, pack_top, pack_bot = solve()

    RS2[0, 0] = PR[0:LEVELS, BASE + ROWS - 2, :]
    RS2[0, 1] = PR[0:LEVELS, BASE + ROWS - 1, :]
    RS2[1, 0] = PR[0:LEVELS, BASE + 1, :]
    RS2[1, 1] = PR[0:LEVELS, BASE, :]
    second = [send(RS2.at[0], RR2.at[0], 1, 0), send(RS2.at[1], RR2.at[1], 1, 1)]
    OWN[0] = pack_top
    OWN[1] = pack_bot
    second += [send(OWN, CR2.at[0], 1, 2), send(OWN, CR2.at[1], 1, 3)]

    lax.fori_loop(0, LEVELS // CHUNK, lift, 0)

    for copy in second:
        copy.wait_recv()

    PR[0:LEVELS, BASE - 1, :] = RR2[0, 1]
    PR[0:LEVELS, BASE + ROWS, :] = RR2[1, 1]
    UR[:, BASE - 1, :] = UR[:, BASE - 1, :] - RR1[0, 2] * (PR[0:LEVELS, BASE, :] - RR2[0, 0])
    UR[:, BASE + ROWS, :] = UR[:, BASE + ROWS, :] - RR1[1, 2] * (
        RR2[1, 0] - PR[0:LEVELS, BASE + ROWS - 1, :]
    )
    for g in range(2):
        from_left = jnp.where(slot < 2, CR2[0, g], NEXT[0, g])
        from_right = jnp.where(slot < 2, NEXT[1, g], CR2[1, g])
        edges(g, from_left, from_right)

    solve()
    stores = [
        pltpu.make_async_copy(UR.at[:, pl.ds(BASE, ROWS), :], u_out, out_sems.at[0]),
        pltpu.make_async_copy(V, v_out, out_sems.at[1]),
        pltpu.make_async_copy(PR.at[pl.ds(0, LEVELS), pl.ds(BASE, ROWS), :], p_out, out_sems.at[2]),
    ]
    for store in stores:
        store.start()
    lax.fori_loop(0, LEVELS // CHUNK, lift, 0)
    store = pltpu.make_async_copy(W.at[pl.ds(1, LEVELS)], w_out, out_sems.at[3])
    store.start()
    for copy in first + second:
        copy.wait_send()
    for store in stores + [store]:
        store.wait()


def per_device(u, v, w, p, c, s):
    block = (LEVELS, ROWS, LANES)
    padded = (LEVELS + 1, 32, LANES)
    pair = (2, ROWS, LANES)
    return pl.pallas_call(
        kernel,
        out_shape=[jax.ShapeDtypeStruct(block, F32)] * 4,
        in_specs=[pl.BlockSpec(memory_space=pl.ANY)] * 6,
        out_specs=[pl.BlockSpec(memory_space=pl.ANY)] * 4,
        scratch_shapes=[
            pltpu.VMEM(padded, F32),
            pltpu.VMEM((LEVELS, 32, LANES), F32),
            pltpu.VMEM(block, F32),
            pltpu.VMEM((LEVELS + 1, ROWS, LANES), F32),
            pltpu.VMEM(block, jnp.bfloat16),
            pltpu.VMEM(block, jnp.bfloat16),
            pltpu.VMEM(block, F32),
            pltpu.VMEM(block, F32),
            pltpu.VMEM(block, F32),
            pltpu.VMEM(block, F32),
            pltpu.VMEM(block, F32),
            pltpu.VMEM((ROWS, LANES), F32),
            pltpu.VMEM((2, 3, LEVELS, LANES), F32),
            pltpu.VMEM((2, 3, LEVELS, LANES), F32),
            pltpu.VMEM((2, 2, LEVELS, LANES), F32),
            pltpu.VMEM((2, 2, LEVELS, LANES), F32),
            pltpu.VMEM((2,) + pair, F32),
            pltpu.VMEM((2,) + pair, F32),
            pltpu.VMEM(pair, F32),
            pltpu.VMEM((2,) + pair, F32),
            pltpu.VMEM(pair, F32),
            pltpu.VMEM(pair, F32),
            pltpu.VMEM((2,) + pair, F32),
            pltpu.SemaphoreType.DMA((6,)),
            pltpu.SemaphoreType.DMA((4,)),
            pltpu.SemaphoreType.DMA((2, 4)),
            pltpu.SemaphoreType.DMA((2, 4)),
        ],
        compiler_params=pltpu.CompilerParams(
            collective_id=0, has_side_effects=True, vmem_limit_bytes=24 * 1024 * 1024
        ),
    )(u, v, w, p, c, s)


def solution(mesh):
    spec = P(None, "rows", "cols")
    return jax.shard_map(
        per_device, mesh=mesh, in_specs=(spec,) * 6, out_specs=(spec,) * 4, check_vma=False
    )
```

profile of v0, /device:TPU:4, one launch (start us, length us, event | category | flops | bytes accessed | tf_op | source)
XLA Modules:
  0.0 45.7 jit_solution(15102602197170358383)
XLA Ops:
  0.6 0.0 copy-start
  0.6 1.0 %copy-done = f32[64,16,128]{2,1,0:T(8,128)S(1)} copy-done((f32[64,16,128]{2,1,0:T(8,128)S(1)}, f32[64,16,128]{2,1,0:T(8,128)}, u32[]{:S(2)}) %copy-start) | copy-done | bytes 524312
  1.7 0.0 copy-start.1
  1.7 1.0 %copy-done.1 = f32[64,16,128]{2,1,0:T(8,128)S(1)} copy-done((f32[64,16,128]{2,1,0:T(8,128)S(1)}, f32[64,16,128]{2,1,0:T(8,128)}, u32[]{:S(2)}) %copy-start.1) | copy-done | bytes 524312
  2.7 0.0 copy-start.2
  2.7 1.0 %copy-done.2 = f32[64,16,128]{2,1,0:T(8,128)S(1)} copy-done((f32[64,16,128]{2,1,0:T(8,128)S(1)}, f32[64,16,128]{2,1,0:T(8,128)}, u32[]{:S(2)}) %copy-start.2) | copy-done | bytes 524312
  3.8 0.0 copy-start.3
  3.8 1.0 %copy-done.3 = f32[64,16,128]{2,1,0:T(8,128)S(1)} copy-done((f32[64,16,128]{2,1,0:T(8,128)S(1)}, f32[64,16,128]{2,1,0:T(8,128)}, u32[]{:S(2)}) %copy-start.3) | copy-done | bytes 524312
  4.8 0.0 copy-start.4
  4.8 0.9 %copy-done.4 = bf16[64,16,128]{2,1,0:T(8,128)(2,1)S(1)} copy-done((bf16[64,16,128]{2,1,0:T(8,128)(2,1)S(1)}, bf16[64,16,128]{2,1,0:T(8,128)(2,1)}, u32[]{:S(2)}) %copy-start.4) | copy-done | bytes 262168
  5.8 0.0 copy-start.5
  5.8 0.9 %copy-done.5 = bf16[64,16,128]{2,1,0:T(8,128)(2,1)S(1)} copy-done((bf16[64,16,128]{2,1,0:T(8,128)(2,1)S(1)}, bf16[64,16,128]{2,1,0:T(8,128)(2,1)}, u32[]{:S(2)}) %copy-start.5) | copy-done | bytes 262168
  6.7 35.8 %shard_map.93 = (f32[64,16,128]{2,1,0:T(8,128)S(1)}, f32[64,16,128]{2,1,0:T(8,128)S(1)}, f32[64,16,128]{2,1,0:T(8,128)S(1)}, f32[64,16,128]{2,1,0:T(8,128)S(1)}) custom-call(f32[64,16,128]{2,1,0:T(8,128)S(1)} %copy-done, f32[64,16,128]{2,1,0:T(8,128)S(1)} %copy-done.1, f32[64,16,128]{2,1,0:T(8,128)S(1)} %copy-done.2, f32[64,16,128]{2,1,0:T(8,128)S(1)} %copy-done.3, ...), custom_call_target="tpu_custom_call" | custom-call | tf_op jit(solution)/shard_map/pallas_call | solution.py:287
  42.5 0.8 %copy.14 = f32[64,16,128]{2,1,0:T(8,128)} copy(f32[64,16,128]{2,1,0:T(8,128)S(1)} %get-tuple-element.8) | data formatting | bytes 1048576
  43.3 0.8 %copy.15 = f32[64,16,128]{2,1,0:T(8,128)} copy(f32[64,16,128]{2,1,0:T(8,128)S(1)} %get-tuple-element.9) | data formatting | bytes 1048576
  44.1 0.8 %copy.16 = f32[64,16,128]{2,1,0:T(8,128)} copy(f32[64,16,128]{2,1,0:T(8,128)S(1)} %get-tuple-element.10) | data formatting | bytes 1048576
  44.9 0.8 %copy.17 = f32[64,16,128]{2,1,0:T(8,128)} copy(f32[64,16,128]{2,1,0:T(8,128)S(1)} %get-tuple-element.11) | data formatting | bytes 1048576
Async XLA Ops:
  0.6 1.0 %copy-start = (f32[64,16,128]{2,1,0:T(8,128)S(1)}, f32[64,16,128]{2,1,0:T(8,128)}, u32[]{:S(2)}) copy-start(f32[64,16,128]{2,1,0:T(8,128)} %u_in.1) | copy-start | bytes 1572868
  1.7 1.0 %copy-start.1 = (f32[64,16,128]{2,1,0:T(8,128)S(1)}, f32[64,16,128]{2,1,0:T(8,128)}, u32[]{:S(2)}) copy-start(f32[64,16,128]{2,1,0:T(8,128)} %v_in.1) | copy-start | bytes 1572868
  2.7 1.0 %copy-start.2 = (f32[64,16,128]{2,1,0:T(8,128)S(1)}, f32[64,16,128]{2,1,0:T(8,128)}, u32[]{:S(2)}) copy-start(f32[64,16,128]{2,1,0:T(8,128)} %w_in.1) | copy-start | bytes 1572868
  3.8 1.0 %copy-start.3 = (f32[64,16,128]{2,1,0:T(8,128)S(1)}, f32[64,16,128]{2,1,0:T(8,128)}, u32[]{:S(2)}) copy-start(f32[64,16,128]{2,1,0:T(8,128)} %p_in.1) | copy-start | bytes 1572868
  4.8 0.9 %copy-start.4 = (bf16[64,16,128]{2,1,0:T(8,128)(2,1)S(1)}, bf16[64,16,128]{2,1,0:T(8,128)(2,1)}, u32[]{:S(2)}) copy-start(bf16[64,16,128]{2,1,0:T(8,128)(2,1)} %c_in.1) | copy-start | bytes 786436
  5.8 0.9 %copy-start.5 = (bf16[64,16,128]{2,1,0:T(8,128)(2,1)S(1)}, bf16[64,16,128]{2,1,0:T(8,128)(2,1)}, u32[]{:S(2)}) copy-start(bf16[64,16,128]{2,1,0:T(8,128)(2,1)} %s_in.1) | copy-start | bytes 786436
where the time goes:
time: 46.1 us; the launch traced here: 45.7 us
  Pallas kernels  35.8 us (78%)
  local copies, waits for them, and re-layouts  9.23 us (20%)
  between operations  0.66 us (1%)
    pallas_call x1, Pallas kernels, per_device(): pl.pallas_call(kernel, out_shape=[jax.ShapeDtypeStruct(block, F32)] * 4,...  35.8 us
    unnamed x16, local copies, waits for them, and re-layouts  9.23 us

commit v1 on v0

v1 whole, which is shorter than its diff:
```python
import jax
import jax.numpy as jnp
from jax import lax
from jax.experimental import pallas as pl
from jax.experimental.pallas import tpu as pltpu
from jax.sharding import PartitionSpec as P

LEVELS = 64
HALF = LEVELS // 2
ROWS = 16
LANES = 128
BASE = 8
CHUNK = 8
STEPS = HALF // CHUNK
PARTS = 4
F32 = jnp.float32
OWN_ROWS = slice(BASE, BASE + ROWS)


def turn(x, shift):
    return pltpu.roll(x, shift % LANES if isinstance(shift, int) else shift, x.ndim - 1)


def rows_of(ref, first):
    stride = ref.shape[1]
    return ref.reshape(ref.shape[0] * stride, LANES), pl.ds(first, LEVELS, stride=stride)


def read_rows(ref, first):
    flat, rows = rows_of(ref, first)
    return flat[rows, :]


def write_rows(ref, first, value):
    flat, rows = rows_of(ref, first)
    flat[rows, :] = value


def marks():
    lane = lax.broadcasted_iota(jnp.int32, (ROWS, LANES), 1)
    return lane, lax.rem(lane, 4), lax.div(lane, 4)


def sweep_in(PR, U_old, U_new, V_old, V_new, W, H, S, E, G, EDGE, Y):
    lane = lax.broadcasted_iota(jnp.int32, (ROWS, LANES), 1)
    first_lane, last_lane = lane == 0, lane == LANES - 1
    zero = jnp.zeros((ROWS, LANES), F32)

    def body(i, carry):
        chain = list(carry)
        for half in range(2):
            k0 = i * CHUNK if half == 0 else LEVELS - CHUNK - i * CHUNK
            ks = pl.ds(k0, CHUNK)
            here = PR[ks, OWN_ROWS, :]
            h = H[ks]
            U_new[ks, OWN_ROWS, :] = U_old[ks, OWN_ROWS, :] - h * (
                PR[ks, BASE + 1 : BASE + ROWS + 1, :] - PR[ks, BASE - 1 : BASE + ROWS - 1, :]
            )
            dv = []
            for j in range(CHUNK):
                kappa = k0 + j - half * HALF
                edge = EDGE[half]
                ep = turn(edge, lax.rem(LANES + 127 - 4 * kappa, LANES))
                ev = turn(edge, lax.rem(LANES + 125 - 4 * kappa, LANES))
                k = k0 + j
                ahead = jnp.where(last_lane, ep, turn(here[j], -1))
                behind = jnp.where(first_lane, ep, turn(here[j], 1))
                v1 = V_old[k] - h[j] * (ahead - behind)
                V_new[k] = v1
                ahead = jnp.where(last_lane, ev, turn(v1, -1))
                behind = jnp.where(first_lane, ev, turn(v1, 1))
                dv.append(ahead - behind)
            du = (
                U_new[ks, BASE + 1 : BASE + ROWS + 1, :]
                - U_new[ks, BASE - 1 : BASE + ROWS - 1, :]
            )
            for j in range(CHUNK) if half == 0 else range(CHUNK - 1, -1, -1):
                k = k0 + j
                source = here[j] - h[j] * (du[j] + dv[j]) - S[k] * (W[k + 1] - W[k])
                chain[half] = E[k] * source + G[k] * chain[half]
                Y[k] = chain[half]
        return tuple(chain)

    return lax.fori_loop(0, STEPS, body, (zero, zero))


def middle(y_top, y_bot, G, M):
    q_bot = (y_bot + G[HALF] * y_top) * M[...]
    q_top = y_top + G[HALF - 1] * q_bot
    return q_bot, q_top


def exchange_kernel(
    u_in, v_in, w_in, p_in, c_in, s_in,
    PR, UR, V, W, H, S, E, G, M, EDGE,
    C16, S16, Y, RS1, RR1, RS2, RR2, CS1, CR1, CR2, OWN, NEXT,
    in_sems, send_sems, recv_sems,
):
    row, col = lax.axis_index("rows"), lax.axis_index("cols")
    nrow, ncol = lax.axis_size("rows"), lax.axis_size("cols")
    up, down = lax.rem(row + 1, nrow), lax.rem(row + nrow - 1, nrow)
    right, left = lax.rem(col + 1, ncol), lax.rem(col + ncol - 1, ncol)
    targets = [(up, col), (down, col), (row, right), (row, left)]

    barrier = pltpu.get_barrier_semaphore()
    for target in targets:
        pl.semaphore_signal(barrier, inc=1, device_id=target, device_id_type=pl.DeviceIdType.MESH)

    loads = [
        pltpu.make_async_copy(c_in, C16, in_sems.at[0]),
        pltpu.make_async_copy(p_in, PR.at[pl.ds(0, LEVELS), pl.ds(BASE, ROWS), :], in_sems.at[1]),
        pltpu.make_async_copy(u_in, UR.at[:, pl.ds(BASE, ROWS), :], in_sems.at[2]),
        pltpu.make_async_copy(v_in, V, in_sems.at[3]),
        pltpu.make_async_copy(s_in, S16, in_sems.at[4]),
        pltpu.make_async_copy(w_in, W.at[pl.ds(1, LEVELS)], in_sems.at[5]),
    ]
    for load in loads:
        load.start()

    zero = jnp.zeros((ROWS, LANES), F32)
    W[0] = zero
    PR[LEVELS, OWN_ROWS, :] = zero
    lane, slot, group = marks()
    ends = (lane == 0) | (lane == LANES - 1)

    loads[0].wait()

    def halve(i, carry):
        k = pl.ds(i * 8, 8)
        H[k] = C16[k].astype(F32) * 0.5
        return carry

    lax.fori_loop(0, LEVELS // 8, halve, 0)

    loads[1].wait()
    loads[2].wait()
    h_lo, h_hi = read_rows(H, 0), read_rows(H, ROWS - 1)
    RS1[0, 0] = read_rows(PR, BASE + ROWS - 1)
    RS1[0, 1] = read_rows(UR, BASE + ROWS - 1) + h_hi * read_rows(PR, BASE + ROWS - 2)
    RS1[0, 2] = h_hi
    RS1[1, 0] = read_rows(PR, BASE)
    RS1[1, 1] = read_rows(UR, BASE) - h_lo * read_rows(PR, BASE + 1)
    RS1[1, 2] = h_lo

    pl.semaphore_wait(barrier, 4)

    def send(source, landing, which, direction):
        copy = pltpu.make_async_remote_copy(
            src_ref=source,
            dst_ref=landing,
            send_sem=send_sems.at[which, direction],
            recv_sem=recv_sems.at[which, direction],
            device_id=targets[direction],
            device_id_type=pl.DeviceIdType.MESH,
        )
        copy.start()
        return copy

    first = [send(RS1.at[0], RR1.at[0], 0, 0), send(RS1.at[1], RR1.at[1], 0, 1)]

    loads[3].wait()

    def pack_first(i, carry):
        out = list(carry)
        for half in range(2):
            for j in range(CHUNK):
                kappa = i * CHUNK + j
                k = half * HALF + kappa
                mask = group == kappa
                pp = turn(PR[k, OWN_ROWS, :], lax.rem(4 * kappa + 2, LANES))
                vh = jnp.where(ends, V[k], turn(H[k], 2))
                vh = turn(vh, lax.rem(4 * kappa + 1, LANES))
                out[half] = jnp.where(mask, pp, out[half])
                out[2 + half] = jnp.where(mask, vh, out[2 + half])
        return tuple(out)

    packed = lax.fori_loop(0, STEPS, pack_first, (zero, zero, zero, zero))
    for g in range(2):
        pp, vh = packed[g], packed[2 + g]
        OWN[g] = pp
        CS1[0, g] = jnp.where(slot < 2, pp, jnp.where(slot == 2, vh, turn(vh, 3)))
        CS1[1, g] = jnp.where(slot == 0, turn(vh, -3), jnp.where(slot == 1, vh, pp))
    first += [send(CS1.at[0], CR1.at[0], 0, 2), send(CS1.at[1], CR1.at[1], 0, 3)]

    loads[4].wait()

    def factor(i, carry):
        above, below = carry
        for j in range(CHUNK):
            k = i * CHUNK + j
            stiff = S16[k].astype(F32)
            S[k] = stiff
            weight = stiff * stiff
            inverse = 1.0 / (1.0 + 2.0 * weight - weight * above)
            above = weight * inverse
            E[k] = inverse
            G[k] = above
            k = LEVELS - 1 - i * CHUNK - j
            stiff = S16[k].astype(F32)
            S[k] = stiff
            weight = stiff * stiff
            inverse = 1.0 / (1.0 + 2.0 * weight - weight * below)
            below = weight * inverse
            E[k] = inverse
            G[k] = below
        return above, below

    above, below = lax.fori_loop(0, STEPS, factor, (zero, zero))
    M[...] = 1.0 / (1.0 - above * below)
    loads[5].wait()

    at_left, at_right = col == 0, col == ncol - 1
    walled = (((slot == 1) | (slot == 3)) & at_left) | (((slot == 0) | (slot == 2)) & at_right)

    def edges(g, from_left, from_right):
        own = OWN[g]
        taken = from_left * (own - turn(from_left, 2))
        v_left = from_left - turn(taken, 1)
        taken = from_right * (turn(from_right, -3) - turn(own, -1))
        v_right = from_right - turn(taken, 1)
        edge = jnp.where(
            slot == 0,
            turn(from_right, -2),
            jnp.where(slot == 1, from_left, jnp.where(slot == 2, turn(v_right, 1), v_left)),
        )
        EDGE[g] = jnp.where(walled, 0.0, edge)
        return v_left, v_right

    for copy in first:
        copy.wait_recv()

    write_rows(PR, BASE - 1, RR1[0, 0])
    write_rows(PR, BASE + ROWS, RR1[1, 0])
    write_rows(UR, BASE - 1, RR1[0, 1] - RR1[0, 2] * read_rows(PR, BASE))
    write_rows(UR, BASE + ROWS, RR1[1, 1] + RR1[1, 2] * read_rows(PR, BASE + ROWS - 1))
    for g in range(2):
        from_left, from_right = CR1[0, g], CR1[1, g]
        v_left, v_right = edges(g, from_left, from_right)
        NEXT[0, g] = jnp.where(slot == 3, v_left, from_left)
        NEXT[1, g] = jnp.where(slot == 1, v_right, from_right)

    y_top, y_bot = sweep_in(PR, UR, UR, V, V, W, H, S, E, G, EDGE, Y)
    q_bot, q_top = middle(y_top, y_bot, G, M)

    def sweep_out(step, carry):
        q_top, q_bot, pack_top, pack_bot = carry
        for j in range(CHUNK):
            k = HALF - 1 - step * CHUNK - j
            q_top = Y[k] + G[k] * q_top
            PR[k, OWN_ROWS, :] = q_top
            pack_top = jnp.where(group == k, turn(q_top, lax.rem(4 * k + 2, LANES)), pack_top)
            kappa = step * CHUNK + j
            k = HALF + kappa
            q_bot = Y[k] + G[k] * q_bot
            PR[k, OWN_ROWS, :] = q_bot
            pack_bot = jnp.where(group == kappa, turn(q_bot, lax.rem(4 * kappa + 2, LANES)), pack_bot)
        return q_top, q_bot, pack_top, pack_bot

    unused, unused, pack_top, pack_bot = lax.fori_loop(
        0, STEPS, sweep_out, (q_bot, q_top, zero, zero)
    )

    RS2[0, 0] = read_rows(PR, BASE + ROWS - 2)
    RS2[0, 1] = read_rows(PR, BASE + ROWS - 1)
    RS2[1, 0] = read_rows(PR, BASE + 1)
    RS2[1, 1] = read_rows(PR, BASE)
    second = [send(RS2.at[0], RR2.at[0], 1, 0), send(RS2.at[1], RR2.at[1], 1, 1)]
    OWN[0] = pack_top
    OWN[1] = pack_bot
    second += [send(OWN, CR2.at[0], 1, 2), send(OWN, CR2.at[1], 1, 3)]

    def lift(i, carry):
        k0 = i * CHUNK
        W[pl.ds(k0 + 1, CHUNK)] = W[pl.ds(k0 + 1, CHUNK)] - S[pl.ds(k0, CHUNK)] * (
            PR[pl.ds(k0 + 1, CHUNK), OWN_ROWS, :] - PR[pl.ds(k0, CHUNK), OWN_ROWS, :]
        )
        return carry

    lax.fori_loop(0, LEVELS // CHUNK, lift, 0)

    for copy in second:
        copy.wait_recv()

    write_rows(PR, BASE - 1, RR2[0, 1])
    write_rows(PR, BASE + ROWS, RR2[1, 1])
    write_rows(
        UR, BASE - 1, read_rows(UR, BASE - 1) - RR1[0, 2] * (read_rows(PR, BASE) - RR2[0, 0])
    )
    write_rows(
        UR,
        BASE + ROWS,
        read_rows(UR, BASE + ROWS) - RR1[1, 2] * (RR2[1, 0] - read_rows(PR, BASE + ROWS - 1)),
    )
    for g in range(2):
        from_left = jnp.where(slot < 2, CR2[0, g], NEXT[0, g])
        from_right = jnp.where(slot < 2, NEXT[1, g], CR2[1, g])
        edges(g, from_left, from_right)
    for copy in first + second:
        copy.wait_send()


def finish_kernel(
    PR, UR, V, W, H, S, E, G, M, EDGE,
    u_out, v_out, w_out, p_out,
    U2, V2, W2, Q, Y, wind_sems, sems,
):
    write_rows(U2, BASE - 1, read_rows(UR, BASE - 1))
    write_rows(U2, BASE + ROWS, read_rows(UR, BASE + ROWS))
    y_top, y_bot = sweep_in(PR, UR, U2, V, V2, W, H, S, E, G, EDGE, Y)
    winds = [
        pltpu.make_async_copy(U2.at[:, pl.ds(BASE, ROWS), :], u_out, wind_sems.at[0]),
        pltpu.make_async_copy(V2, v_out, wind_sems.at[1]),
    ]
    for copy in winds:
        copy.start()
    q_bot, q_top = middle(y_top, y_bot, G, M)

    def sweep_out(step, carry):
        q_top, q_bot = carry
        for j in range(CHUNK):
            k = HALF - 1 - step * CHUNK - j
            q_next = q_top
            q_top = Y[k] + G[k] * q_next
            Q[k] = q_top
            W2[k] = W[k + 1] - S[k] * (q_next - q_top)
            k = HALF + step * CHUNK + j
            q_before = q_bot
            q_bot = Y[k] + G[k] * q_before
            Q[k] = q_bot
            W2[k - 1] = W[k] - S[k - 1] * (q_bot - q_before)
        return q_top, q_bot

    carry = q_bot, q_top
    copies = []
    part = HALF // PARTS
    for n in range(PARTS):
        carry = lax.fori_loop(n * STEPS // PARTS, (n + 1) * STEPS // PARTS, sweep_out, carry)
        low, high = HALF - (n + 1) * part, HALF + n * part
        spans = [(Q, p_out, low, low + part), (Q, p_out, high, high + part), (W2, w_out, low, low + part)]
        start, stop = max(HALF, high - 1), high + part - 1
        if n == PARTS - 1:
            W2[LEVELS - 1] = W[LEVELS] + S[LEVELS - 1] * carry[1]
            stop = LEVELS
        spans.append((W2, w_out, start, stop))
        for m, (source, target, begin, end) in enumerate(spans):
            ks = pl.ds(begin, end - begin)
            copy = pltpu.make_async_copy(source.at[ks], target.at[ks], sems.at[n, m])
            copy.start()
            copies.append(copy)
    for copy in winds + copies:
        copy.wait()


def per_device(u, v, w, p, c, s):
    block = (LEVELS, ROWS, LANES)
    padded = (LEVELS, 2 * ROWS, LANES)
    plane = (ROWS, LANES)
    pair = (2, ROWS, LANES)
    vmem = pl.BlockSpec(memory_space=pltpu.VMEM)
    hbm = pl.BlockSpec(memory_space=pltpu.HBM)
    state = [
        (LEVELS + 1, 2 * ROWS, LANES), padded, block, (LEVELS + 1, ROWS, LANES),
        block, block, block, block, plane, pair,
    ]
    held = pl.pallas_call(
        exchange_kernel,
        out_shape=[jax.ShapeDtypeStruct(shape, F32) for shape in state],
        in_specs=[hbm] * 6,
        out_specs=[vmem] * len(state),
        scratch_shapes=[
            pltpu.VMEM(block, jnp.bfloat16),
            pltpu.VMEM(block, jnp.bfloat16),
            pltpu.VMEM(block, F32),
            pltpu.VMEM((2, 3, LEVELS, LANES), F32),
            pltpu.VMEM((2, 3, LEVELS, LANES), F32),
            pltpu.VMEM((2, 2, LEVELS, LANES), F32),
            pltpu.VMEM((2, 2, LEVELS, LANES), F32),
            pltpu.VMEM((2,) + pair, F32),
            pltpu.VMEM((2,) + pair, F32),
            pltpu.VMEM((2,) + pair, F32),
            pltpu.VMEM(pair, F32),
            pltpu.VMEM((2,) + pair, F32),
            pltpu.SemaphoreType.DMA((6,)),
            pltpu.SemaphoreType.DMA((2, 4)),
            pltpu.SemaphoreType.DMA((2, 4)),
        ],
        compiler_params=pltpu.CompilerParams(
            collective_id=0, has_side_effects=True, vmem_limit_bytes=16 * 1024 * 1024
        ),
    )(*[pltpu.with_memory_space_constraint(x, pltpu.HBM) for x in (u, v, w, p, c, s)])
    return pl.pallas_call(
        finish_kernel,
        out_shape=[jax.ShapeDtypeStruct(block, F32)] * 4,
        in_specs=[vmem] * len(state),
        out_specs=[hbm] * 4,
        scratch_shapes=[
            pltpu.VMEM(padded, F32),
            pltpu.VMEM(block, F32),
            pltpu.VMEM(block, F32),
            pltpu.VMEM(block, F32),
            pltpu.VMEM(block, F32),
            pltpu.SemaphoreType.DMA((2,)),
            pltpu.SemaphoreType.DMA((PARTS, 4)),
        ],
        compiler_params=pltpu.CompilerParams(vmem_limit_bytes=16 * 1024 * 1024),
    )(*held)


def solution(mesh):
    spec = P(None, "rows", "cols")
    return jax.shard_map(
        per_device, mesh=mesh, in_specs=(spec,) * 6, out_specs=(spec,) * 4, check_vma=False
    )
```

time: 46.1 us -> 37.3 us (0.81)
  the two profiles are of different devices: /device:TPU:4 before, /device:TPU:6 now
where the time goes in v1:
time: 37.3 us; the launch traced here: 36.6 us
  Pallas kernels  35.9 us (96%)
  between operations  0.64 us (2%)
    pallas_call x1, Pallas kernels, per_device(): pl.pallas_call(exchange_kernel, out_shape=[jax.ShapeDtypeStruct(shape, F3...  32.4 us
    pallas_call x1, Pallas kernels, per_device(): pl.pallas_call(finish_kernel, out_shape=[jax.ShapeDtypeStruct(block, F32)...  3.57 us

profile of v1, /device:TPU:6, one launch (start us, length us, event | category | flops | bytes accessed | tf_op | source)
XLA Modules:
  0.0 36.6 jit_solution(7025362553882226354)
XLA Ops:
  0.6 32.4 %shard_map.93 = (f32[65,32,128]{2,1,0:T(8,128)S(1)}, f32[64,32,128]{2,1,0:T(8,128)S(1)}, f32[64,16,128]{2,1,0:T(8,128)S(1)}, f32[65,16,128]{2,1,0:T(8,128)S(1)},...) custom-call(f32[64,16,128]{2,1,0:T(8,128)} %u_in.1, ...), custom_call_target="tpu_custom_call" | custom-call | tf_op jit(solution)/shard_map/pallas_call | solution.py:365
  33.0 3.6 %shard_map.94 = (f32[64,16,128]{2,1,0:T(8,128)}, f32[64,16,128]{2,1,0:T(8,128)}, f32[64,16,128]{2,1,0:T(8,128)}, f32[64,16,128]{2,1,0:T(8,128)}) custom-call(f32[65,32,128]{2,1,0:T(8,128)S(1)} %get-tuple-element.14.PR, f32[64,32,128]{2,1,0:T(8,128)S(1)} %get-tuple-element.15.UR, f32[64,16,128]{2,1,0:T(8,128)S(1)} %get-tuple-element.16.V, ...), custom_call_target="tpu_custom_call" | custom-call | tf_op jit(solution)/shard_map/pallas_call | solution.py:391

commit v2 on v1

v2 whole, which is shorter than its diff:
```python
import jax
import jax.numpy as jnp
from jax import lax
from jax.experimental import pallas as pl
from jax.experimental.pallas import tpu as pltpu
from jax.sharding import PartitionSpec as P

LEVELS = 64
HALF = LEVELS // 2
ROWS = 16
LANES = 128
BASE = 8
CHUNK = 8
STEPS = HALF // CHUNK
PIECES = 2
DEPTH = HALF // PIECES
PARTS = 4
F32 = jnp.float32
OWN_ROWS = slice(BASE, BASE + ROWS)
PLANE = (ROWS, LANES)
MESH = pl.DeviceIdType.MESH


def turn(x, shift):
    return pltpu.roll(x, shift % LANES if isinstance(shift, int) else shift, x.ndim - 1)


def rows_of(ref, row, level, count):
    stride = ref.shape[1]
    return ref.reshape(ref.shape[0] * stride, LANES), pl.ds(level * stride + row, count, stride=stride)


def read_rows(ref, row, level=0, count=LEVELS):
    flat, rows = rows_of(ref, row, level, count)
    return flat[rows, :]


def write_rows(ref, row, value, level=0, count=LEVELS):
    flat, rows = rows_of(ref, row, level, count)
    flat[rows, :] = value


def edge_lanes(lane, inside):
    return (lane >= LANES - inside) | (lane < inside)


def eliminate(steps, carry, SRC, E, G, CORR, Y, V=None, VC=None, V2=None):
    lane = lax.broadcasted_iota(jnp.int32, PLANE, 1)
    near, nearest = edge_lanes(lane, 2), edge_lanes(lane, 1)

    def body(i, carry):
        chain = list(carry)
        for j in range(CHUNK):
            for half in range(2):
                k = LEVELS - 1 - i * CHUNK - j if half else i * CHUNK + j
                shift = lax.rem(2 * LANES - 4 * (k - half * HALF) - 2, LANES)
                source = SRC[k] + jnp.where(near, turn(CORR[half], shift), 0.0)
                chain[half] = E[k] * source + G[k] * chain[half]
                Y[k] = chain[half]
                if V is not None:
                    V2[k] = V[k] + jnp.where(nearest, turn(VC[half], shift), 0.0)
        return tuple(chain)

    return lax.fori_loop(*steps, body, carry)


def middle(y_top, y_bot, G, M):
    q_bot = (y_bot + G[HALF] * y_top) * M[...]
    q_top = y_top + G[HALF - 1] * q_bot
    return q_bot, q_top


def exchange_kernel(
    u_in, v_in, w_in, p_in, c_in, s_in,
    UR, V, W, S, SRC, E, G, M, CORR, VC,
    PR, H, C16, S16, Y, RS1, RR1, RS2, RR2, UH, CS1, CR1, CS2, CR2, OWN, HC, EDGE,
    in_sems, row_send1, row_recv1, col_send1, col_recv1, send2, recv2,
):
    row, col = lax.axis_index("rows"), lax.axis_index("cols")
    nrow, ncol = lax.axis_size("rows"), lax.axis_size("cols")
    up, down = lax.rem(row + 1, nrow), lax.rem(row + nrow - 1, nrow)
    right, left = lax.rem(col + 1, ncol), lax.rem(col + ncol - 1, ncol)
    targets = [(up, col), (down, col), (row, right), (row, left)]

    barrier = pltpu.get_barrier_semaphore()
    for target in targets:
        pl.semaphore_signal(barrier, inc=1, device_id=target, device_id_type=MESH)

    loads = [
        pltpu.make_async_copy(c_in, C16, in_sems.at[0]),
        pltpu.make_async_copy(p_in, PR.at[pl.ds(0, LEVELS), pl.ds(BASE, ROWS), :], in_sems.at[1]),
        pltpu.make_async_copy(u_in, UR.at[:, pl.ds(BASE, ROWS), :], in_sems.at[2]),
        pltpu.make_async_copy(v_in, V, in_sems.at[3]),
        pltpu.make_async_copy(s_in, S16, in_sems.at[4]),
        pltpu.make_async_copy(w_in, W.at[pl.ds(1, LEVELS)], in_sems.at[5]),
    ]
    for load in loads:
        load.start()

    zero = jnp.zeros(PLANE, F32)
    W[0] = zero
    PR[LEVELS, OWN_ROWS, :] = zero
    no_rows = jnp.zeros((LEVELS, LANES), F32)
    for ref in (PR, UR):
        write_rows(ref, BASE - 1, no_rows)
        write_rows(ref, BASE + ROWS, no_rows)
    lane = lax.broadcasted_iota(jnp.int32, PLANE, 1)
    slot, group = lax.rem(lane, 4), lax.div(lane, 4)
    outer, inner = (slot == 0) | (slot == 3), (slot == 1) | (slot == 2)

    loads[0].wait()

    def halve(i, carry):
        k = pl.ds(i * 8, 8)
        H[k] = C16[k].astype(F32) * 0.5
        return carry

    lax.fori_loop(0, LEVELS // 8, halve, 0)

    loads[1].wait()
    loads[2].wait()

    def send(source, landing, send_sem, recv_sem, direction):
        copy = pltpu.make_async_remote_copy(
            src_ref=source,
            dst_ref=landing,
            send_sem=send_sem,
            recv_sem=recv_sem,
            device_id=targets[direction],
            device_id_type=MESH,
        )
        copy.start()
        return copy

    def spans(n):
        return ((0, n * DEPTH), (1, LEVELS - (n + 1) * DEPTH))

    top = BASE + ROWS - 1
    row_copies = []
    for n in range(PIECES):
        for half, k0 in spans(n):
            h_lo, h_hi = read_rows(H, 0, k0, DEPTH), read_rows(H, ROWS - 1, k0, DEPTH)
            RS1[0, n, half, 0] = read_rows(PR, top, k0, DEPTH)
            RS1[0, n, half, 1] = read_rows(UR, top, k0, DEPTH) + h_hi * read_rows(PR, top - 1, k0, DEPTH)
            RS1[0, n, half, 2] = h_hi
            RS1[1, n, half, 0] = read_rows(PR, BASE, k0, DEPTH)
            RS1[1, n, half, 1] = read_rows(UR, BASE, k0, DEPTH) - h_lo * read_rows(PR, BASE + 1, k0, DEPTH)
            RS1[1, n, half, 2] = h_lo
        if n == 0:
            pl.semaphore_wait(barrier, 4)
        row_copies.append(
            [
                send(RS1.at[d, n], RR1.at[d, n], row_send1.at[d, n], row_recv1.at[d, n], d)
                for d in range(2)
            ]
        )

    loads[3].wait()

    def pack_first(i, carry):
        out = list(carry)
        for half in range(2):
            for j in range(CHUNK):
                kappa = i * CHUNK + j
                k = half * HALF + kappa
                mask = group == kappa
                shift = lax.rem(4 * kappa + 2, LANES)
                for n, field in enumerate((PR[k, OWN_ROWS, :], V[k], H[k])):
                    out[2 * n + half] = jnp.where(mask, turn(field, shift), out[2 * n + half])
        return tuple(out)

    packed = lax.fori_loop(0, STEPS, pack_first, (zero,) * 6)
    for g in range(2):
        pp, vp, hp = packed[g], packed[2 + g], packed[4 + g]
        OWN[g] = pp
        px = jnp.where(slot < 2, turn(pp, -2), turn(pp, 2))
        vx = jnp.where(slot < 2, turn(vp, -1), turn(vp, 1))
        hx = jnp.where(slot == 1, turn(hp, -1), jnp.where(slot == 2, -turn(hp, 1), 0.0))
        CS1[0, g] = jnp.where(inner, vx - hx * px, px)
        CS1[1, g] = hx
        HC[g] = jnp.where(
            slot == 0,
            hp * turn(hp, -1),
            jnp.where(slot == 1, -hp, jnp.where(slot == 2, hp, hp * turn(hp, 1))),
        )
    col_copies = [
        send(CS1, CR1.at[d], col_send1.at[d], col_recv1.at[d], 2 + d) for d in range(2)
    ]

    loads[4].wait()

    def factor(i, carry):
        ratios = list(carry)
        for j in range(CHUNK):
            for half in range(2):
                k = LEVELS - 1 - i * CHUNK - j if half else i * CHUNK + j
                stiff = S16[k].astype(F32)
                S[k] = stiff
                weight = stiff * stiff
                inverse = 1.0 / (1.0 + 2.0 * weight - weight * ratios[half])
                ratios[half] = weight * inverse
                E[k] = inverse
                G[k] = ratios[half]
        return tuple(ratios)

    above, below = lax.fori_loop(0, STEPS, factor, (zero, zero))
    M[...] = 1.0 / (1.0 - above * below)
    loads[5].wait()

    span = 4
    wide_lane = lax.broadcasted_iota(jnp.int32, (span,) + PLANE, 2)
    first_lane, last_lane = wide_lane == 0, wide_lane == LANES - 1

    def across(x):
        return jnp.where(last_lane, 0.0, turn(x, -1)) - jnp.where(first_lane, 0.0, turn(x, 1))

    def inside(i, carry):
        ks = pl.ds(i * span, span)
        here, h = PR[ks, OWN_ROWS, :], H[ks]
        UR[ks, OWN_ROWS, :] = UR[ks, OWN_ROWS, :] - h * (
            PR[ks, BASE + 1 : BASE + ROWS + 1, :] - PR[ks, BASE - 1 : BASE + ROWS - 1, :]
        )
        v_new = V[ks] - h * across(here)
        V[ks] = v_new
        du = UR[ks, BASE + 1 : BASE + ROWS + 1, :] - UR[ks, BASE - 1 : BASE + ROWS - 1, :]
        lifted = S[ks] * (W[pl.ds(i * span + 1, span)] - W[ks])
        SRC[ks] = here - h * (du + across(v_new)) - lifted
        return carry

    lax.fori_loop(0, LEVELS // span, inside, 0)

    at_left, at_right = col == 0, col == ncol - 1
    walled = ((slot >= 2) & at_left) | ((slot < 2) & at_right)

    def row_effects(k0, count, p_below, p_above, u_below, u_above):
        h_lo, h_hi = read_rows(H, 0, k0, count), read_rows(H, ROWS - 1, k0, count)
        lo, hi = h_lo * p_below, h_hi * p_above
        changes = (
            (0, h_lo * u_below),
            (1, read_rows(H, 1, k0, count) * lo),
            (ROWS - 2, read_rows(H, ROWS - 2, k0, count) * hi),
            (ROWS - 1, -h_hi * u_above),
        )
        for r, change in changes:
            write_rows(SRC, r, read_rows(SRC, r, k0, count) + change, k0, count)
        write_rows(UR, BASE, read_rows(UR, BASE, k0, count) + lo, k0, count)
        write_rows(UR, top, read_rows(UR, top, k0, count) - hi, k0, count)

    def col_effects(g, edge):
        CORR[g] = HC[g] * edge
        VC[g] = HC[g] * jnp.where(slot == 1, turn(edge, 1), turn(edge, -1))

    chain = (zero, zero)
    for n in range(PIECES):
        for copy in row_copies[n]:
            copy.wait_recv()
        for half, k0 in spans(n):
            levels = pl.ds(k0, DEPTH)
            u_below = RR1[0, n, half, 1] - RR1[0, n, half, 2] * read_rows(PR, BASE, k0, DEPTH)
            u_above = RR1[1, n, half, 1] + RR1[1, n, half, 2] * read_rows(PR, top, k0, DEPTH)
            UH[0, levels] = u_below
            UH[1, levels] = u_above
            row_effects(k0, DEPTH, RR1[0, n, half, 0], RR1[1, n, half, 0], u_below, u_above)
        if n == 0:
            for copy in col_copies:
                copy.wait_recv()
            for g in range(2):
                base = jnp.where(slot < 2, CR1[1, 0, g], CR1[0, 0, g])
                hx = jnp.where(slot < 2, CR1[1, 1, g], CR1[0, 1, g])
                edge = jnp.where(walled, 0.0, base + hx * OWN[g])
                EDGE[g] = edge
                col_effects(g, edge)
        chain = eliminate((n * STEPS // PIECES, (n + 1) * STEPS // PIECES), chain, SRC, E, G, CORR, Y)
    q_bot, q_top = middle(*chain, G, M)

    def substitute(step, carry):
        q_top, q_bot, pack_top, pack_bot = carry
        for j in range(CHUNK):
            k = HALF - 1 - step * CHUNK - j
            q_top = Y[k] + G[k] * q_top
            PR[k, OWN_ROWS, :] = q_top
            pack_top = jnp.where(group == k, turn(q_top, lax.rem(4 * k + 2, LANES)), pack_top)
            kappa = step * CHUNK + j
            k = HALF + kappa
            q_bot = Y[k] + G[k] * q_bot
            PR[k, OWN_ROWS, :] = q_bot
            pack_bot = jnp.where(group == kappa, turn(q_bot, lax.rem(4 * kappa + 2, LANES)), pack_bot)
        return q_top, q_bot, pack_top, pack_bot

    unused, unused, pack_top, pack_bot = lax.fori_loop(
        0, STEPS, substitute, (q_bot, q_top, zero, zero)
    )

    RS2[0, 0] = read_rows(PR, top - 1)
    RS2[0, 1] = read_rows(PR, top)
    RS2[1, 0] = read_rows(PR, BASE + 1)
    RS2[1, 1] = read_rows(PR, BASE)
    second = [send(RS2.at[d], RR2.at[d], send2.at[d], recv2.at[d], d) for d in range(2)]
    for g, pack in enumerate((pack_top, pack_bot)):
        OWN[g] = pack
        CS2[g] = jnp.where(slot < 2, turn(pack, -2), turn(pack, 2))
    second += [send(CS2, CR2.at[d], send2.at[2 + d], recv2.at[2 + d], 2 + d) for d in range(2)]

    nearest = edge_lanes(lane, 1)

    def settle(i, carry):
        for j in range(CHUNK):
            for half in range(2):
                kappa = i * CHUNK + j
                k = half * HALF + kappa
                shift = lax.rem(2 * LANES - 4 * kappa - 2, LANES)
                V[k] = V[k] + jnp.where(nearest, turn(VC[half], shift), 0.0)
                W[k + 1] = W[k + 1] - S[k] * (PR[k + 1, OWN_ROWS, :] - PR[k, OWN_ROWS, :])
        return carry

    lax.fori_loop(0, STEPS, settle, 0)
    lax.fori_loop(0, LEVELS // span, inside, 0)

    for copy in second:
        copy.wait_recv()

    hb, ha = [
        jnp.concatenate([RR1[d, n, half, 2] for n, half in ORDER], axis=0) for d in range(2)
    ]
    u_below = UH[0] - hb * (read_rows(PR, BASE) - RR2[0, 0])
    u_above = UH[1] + ha * (read_rows(PR, top) - RR2[1, 0])
    row_effects(0, LEVELS, RR2[0, 1], RR2[1, 1], u_below, u_above)
    for g in range(2):
        hx = jnp.where(slot < 2, CR1[1, 1, g], CR1[0, 1, g])
        qx = jnp.where(slot < 2, CR2[1, g], CR2[0, g])
        edge = jnp.where(inner, EDGE[g] + hx * (OWN[g] - qx), qx)
        col_effects(g, jnp.where(walled, 0.0, edge))
    for copy in sum(row_copies, col_copies + second):
        copy.wait_send()


ORDER = [(n, 0) for n in range(PIECES)] + [(n, 1) for n in reversed(range(PIECES))]


def finish_kernel(
    UR, V, W, S, SRC, E, G, M, CORR, VC,
    u_out, v_out, w_out, p_out,
    V2, W2, Q, Y, wind_sems, sems,
):
    winds = [
        pltpu.make_async_copy(UR.at[:, pl.ds(BASE, ROWS), :], u_out, wind_sems.at[0]),
        pltpu.make_async_copy(V2, v_out, wind_sems.at[1]),
    ]
    winds[0].start()
    zero = jnp.zeros(PLANE, F32)
    y_top, y_bot = eliminate((0, STEPS), (zero, zero), SRC, E, G, CORR, Y, V, VC, V2)
    winds[1].start()
    q_bot, q_top = middle(y_top, y_bot, G, M)

    def sweep_out(step, carry):
        q_top, q_bot = carry
        for j in range(CHUNK):
            k = HALF - 1 - step * CHUNK - j
            q_next = q_top
            q_top = Y[k] + G[k] * q_next
            Q[k] = q_top
            W2[k] = W[k + 1] - S[k] * (q_next - q_top)
            k = HALF + step * CHUNK + j
            q_before = q_bot
            q_bot = Y[k] + G[k] * q_before
            Q[k] = q_bot
            W2[k - 1] = W[k] - S[k - 1] * (q_bot - q_before)
        return q_top, q_bot

    carry = q_bot, q_top
    copies = []
    part = HALF // PARTS
    for n in range(PARTS):
        carry = lax.fori_loop(n * STEPS // PARTS, (n + 1) * STEPS // PARTS, sweep_out, carry)
        low, high = HALF - (n + 1) * part, HALF + n * part
        start, stop = max(HALF, high - 1), high + part - 1
        if n == PARTS - 1:
            W2[LEVELS - 1] = W[LEVELS] + S[LEVELS - 1] * carry[1]
            stop = LEVELS
        pieces = (
            (Q, p_out, low, low + part),
            (Q, p_out, high, high + part),
            (W2, w_out, low, low + part),
            (W2, w_out, start, stop),
        )
        for m, (source, target, begin, end) in enumerate(pieces):
            ks = pl.ds(begin, end - begin)
            copy = pltpu.make_async_copy(source.at[ks], target.at[ks], sems.at[n, m])
            copy.start()
            copies.append(copy)
    for copy in winds + copies:
        copy.wait()


def per_device(u, v, w, p, c, s):
    block = (LEVELS,) + PLANE
    deep = (LEVELS + 1,) + PLANE
    padded = (LEVELS, 2 * ROWS, LANES)
    pair = (2,) + PLANE
    vmem = pl.BlockSpec(memory_space=pltpu.VMEM)
    hbm = pl.BlockSpec(memory_space=pltpu.HBM)
    state = [padded, block, deep, block, block, block, block, PLANE, pair, pair]
    rows1 = (2, PIECES, 2, 3, DEPTH, LANES)
    rows2 = (2, 2, LEVELS, LANES)
    dma = pltpu.SemaphoreType.DMA
    held = pl.pallas_call(
        exchange_kernel,
        out_shape=[jax.ShapeDtypeStruct(shape, F32) for shape in state],
        in_specs=[hbm] * 6,
        out_specs=[vmem] * len(state),
        scratch_shapes=[
            pltpu.VMEM((LEVELS + 1, 2 * ROWS, LANES), F32),
            pltpu.VMEM(block, F32),
            pltpu.VMEM(block, jnp.bfloat16),
            pltpu.VMEM(block, jnp.bfloat16),
            pltpu.VMEM(block, F32),
            pltpu.VMEM(rows1, F32),
            pltpu.VMEM(rows1, F32),
            pltpu.VMEM(rows2, F32),
            pltpu.VMEM(rows2, F32),
            pltpu.VMEM((2, LEVELS, LANES), F32),
            pltpu.VMEM((2,) + pair, F32),
            pltpu.VMEM((2, 2) + pair, F32),
            pltpu.VMEM(pair, F32),
            pltpu.VMEM((2,) + pair, F32),
            pltpu.VMEM(pair, F32),
            pltpu.VMEM(pair, F32),
            pltpu.VMEM(pair, F32),
            dma((6,)),
            dma((2, PIECES)),
            dma((2, PIECES)),
            dma((2,)),
            dma((2,)),
            dma((4,)),
            dma((4,)),
        ],
        compiler_params=pltpu.CompilerParams(
            collective_id=0, has_side_effects=True, vmem_limit_bytes=16 * 1024 * 1024
        ),
    )(*[pltpu.with_memory_space_constraint(x, pltpu.HBM) for x in (u, v, w, p, c, s)])
    return pl.pallas_call(
        finish_kernel,
        out_shape=[jax.ShapeDtypeStruct(block, F32)] * 4,
        in_specs=[vmem] * len(state),
        out_specs=[hbm] * 4,
        scratch_shapes=[
            pltpu.VMEM(block, F32),
            pltpu.VMEM(block, F32),
            pltpu.VMEM(block, F32),
            pltpu.VMEM(block, F32),
            dma((2,)),
            dma((PARTS, 4)),
        ],
        compiler_params=pltpu.CompilerParams(vmem_limit_bytes=16 * 1024 * 1024),
    )(*held)


def solution(mesh):
    spec = P(None, "rows", "cols")
    return jax.shard_map(
        per_device, mesh=mesh, in_specs=(spec,) * 6, out_specs=(spec,) * 4, check_vma=False
    )
```

time: 37.3 us -> 33.2 us (0.89); the launches traced: 36.6 us -> 33 us
  Pallas kernels: 35.9 us -> 32.3 us
    pallas_call x1, Pallas kernels: 32.4 us -> 30.5 us  [per_device(): pl.pallas_call(exchange_kernel, out_shape=[jax.ShapeDtypeStruct(shape, F3...]
    pallas_call x1, Pallas kernels: 3.57 us -> 1.85 us  [per_device(): pl.pallas_call(finish_kernel, out_shape=[jax.ShapeDtypeStruct(block, F32)...]
where the time goes in v2:
time: 33.2 us; the launch traced here: 33 us
  Pallas kernels  32.3 us (97%)
  between operations  0.64 us (2%)
    pallas_call x1, Pallas kernels, per_device(): pl.pallas_call(exchange_kernel, out_shape=[jax.ShapeDtypeStruct(shape, F3...  30.5 us
    pallas_call x1, Pallas kernels, per_device(): pl.pallas_call(finish_kernel, out_shape=[jax.ShapeDtypeStruct(block, F32)...  1.85 us

profile of v2, /device:TPU:6, one launch (start us, length us, event | category | flops | bytes accessed | tf_op | source)
XLA Modules:
  0.0 33.0 jit_solution(14454034922301241398)
XLA Ops:
  0.6 30.5 %shard_map.93 = (f32[64,32,128]{2,1,0:T(8,128)S(1)}, f32[64,16,128]{2,1,0:T(8,128)S(1)}, f32[65,16,128]{2,1,0:T(8,128)S(1)}, f32[64,16,128]{2,1,0:T(8,128)S(1)},...) custom-call(f32[64,16,128]{2,1,0:T(8,128)} %u_in.1, ...), custom_call_target="tpu_custom_call" | custom-call | tf_op jit(solution)/shard_map/pallas_call | solution.py:406
  31.1 1.8 %shard_map.94 = (f32[64,16,128]{2,1,0:T(8,128)}, f32[64,16,128]{2,1,0:T(8,128)}, f32[64,16,128]{2,1,0:T(8,128)}, f32[64,16,128]{2,1,0:T(8,128)}) custom-call(f32[64,32,128]{2,1,0:T(8,128)S(1)} %get-tuple-element.14.UR, f32[64,16,128]{2,1,0:T(8,128)S(1)} %get-tuple-element.15.V, f32[65,16,128]{2,1,0:T(8,128)S(1)} %get-tuple-element.16.W, ...), custom_call_target="tpu_custom_call" | custom-call | tf_op jit(solution)/shard_map/pallas_call | solution.py:441

commit v3 on v2

--- a/solution.py
+++ b/solution.py
@@ -12,8 +12,8 @@
 BASE = 8
 CHUNK = 8
 STEPS = HALF // CHUNK
-PIECES = 2
-DEPTH = HALF // PIECES
+PIECES = 4
+PIECES2 = 2
 PARTS = 4
 F32 = jnp.float32
 OWN_ROWS = slice(BASE, BASE + ROWS)
@@ -44,9 +44,9 @@
     return (lane >= LANES - inside) | (lane < inside)
 
 
-def eliminate(steps, carry, SRC, E, G, CORR, Y, V=None, VC=None, V2=None):
+def eliminate(steps, carry, SRC, E, G, CORR, Y):
     lane = lax.broadcasted_iota(jnp.int32, PLANE, 1)
-    near, nearest = edge_lanes(lane, 2), edge_lanes(lane, 1)
+    near = edge_lanes(lane, 2)
 
     def body(i, carry):
         chain = list(carry)
@@ -57,8 +57,6 @@
                 source = SRC[k] + jnp.where(near, turn(CORR[half], shift), 0.0)
                 chain[half] = E[k] * source + G[k] * chain[half]
                 Y[k] = chain[half]
-                if V is not None:
-                    V2[k] = V[k] + jnp.where(nearest, turn(VC[half], shift), 0.0)
         return tuple(chain)
 
     return lax.fori_loop(*steps, body, carry)
@@ -72,9 +70,10 @@
 
 def exchange_kernel(
     u_in, v_in, w_in, p_in, c_in, s_in,
-    UR, V, W, S, SRC, E, G, M, CORR, VC,
-    PR, H, C16, S16, Y, RS1, RR1, RS2, RR2, UH, CS1, CR1, CS2, CR2, OWN, HC, EDGE,
-    in_sems, row_send1, row_recv1, col_send1, col_recv1, send2, recv2,
+    UR, V, W, S, Y, G, M,
+    PR, H, C16, S16, SRC, E, CORR, VC, RS1, RR1, RS2, RR2, UH, HH,
+    CS1, CR1, CS2, CR2, OWN, HC, HX, EDGE,
+    in_sems, row_send1, row_recv1, col_send1, col_recv1, row_send2, row_recv2, col_send2, col_recv2,
 ):
     row, col = lax.axis_index("rows"), lax.axis_index("cols")
     nrow, ncol = lax.axis_size("rows"), lax.axis_size("cols")
@@ -132,28 +131,20 @@
         copy.start()
         return copy
 
-    def spans(n):
-        return ((0, n * DEPTH), (1, LEVELS - (n + 1) * DEPTH))
+    def spans(n, depth):
+        return ((0, n * depth), (1, LEVELS - (n + 1) * depth))
 
     top = BASE + ROWS - 1
-    row_copies = []
+    depth = HALF // PIECES
     for n in range(PIECES):
-        for half, k0 in spans(n):
-            h_lo, h_hi = read_rows(H, 0, k0, DEPTH), read_rows(H, ROWS - 1, k0, DEPTH)
-            RS1[0, n, half, 0] = read_rows(PR, top, k0, DEPTH)
-            RS1[0, n, half, 1] = read_rows(UR, top, k0, DEPTH) + h_hi * read_rows(PR, top - 1, k0, DEPTH)
+        for half, k0 in spans(n, depth):
+            h_lo, h_hi = read_rows(H, 0, k0, depth), read_rows(H, ROWS - 1, k0, depth)
+            RS1[0, n, half, 0] = read_rows(PR, top, k0, depth)
+            RS1[0, n, half, 1] = read_rows(UR, top, k0, depth) + h_hi * read_rows(PR, top - 1, k0, depth)
             RS1[0, n, half, 2] = h_hi
-            RS1[1, n, half, 0] = read_rows(PR, BASE, k0, DEPTH)
-            RS1[1, n, half, 1] = read_rows(UR, BASE, k0, DEPTH) - h_lo * read_rows(PR, BASE + 1, k0, DEPTH)
+            RS1[1, n, half, 0] = read_rows(PR, BASE, k0, depth)
+            RS1[1, n, half, 1] = read_rows(UR, BASE, k0, depth) - h_lo * read_rows(PR, BASE + 1, k0, depth)
             RS1[1, n, half, 2] = h_lo
-        if n == 0:
-            pl.semaphore_wait(barrier, 4)
-        row_copies.append(
-            [
-                send(RS1.at[d, n], RR1.at[d, n], row_send1.at[d, n], row_recv1.at[d, n], d)
-                for d in range(2)
-            ]
-        )
 
     loads[3].wait()
 
@@ -176,15 +167,22 @@
         px = jnp.where(slot < 2, turn(pp, -2), turn(pp, 2))
         vx = jnp.where(slot < 2, turn(vp, -1), turn(vp, 1))
         hx = jnp.where(slot == 1, turn(hp, -1), jnp.where(slot == 2, -turn(hp, 1), 0.0))
-        CS1[0, g] = jnp.where(inner, vx - hx * px, px)
-        CS1[1, g] = hx
+        base = jnp.where(inner, vx - hx * px, px)
+        CS1[0, g] = jnp.where(slot == 1, turn(hx, -1), base)
+        CS1[1, g] = jnp.where(slot == 2, turn(hx, 1), base)
         HC[g] = jnp.where(
             slot == 0,
             hp * turn(hp, -1),
             jnp.where(slot == 1, -hp, jnp.where(slot == 2, hp, hp * turn(hp, 1))),
         )
+
+    pl.semaphore_wait(barrier, 4)
+    row_copies = [
+        [send(RS1.at[d, n], RR1.at[d, n], row_send1.at[d, n], row_recv1.at[d, n], d) for d in range(2)]
+        for n in range(PIECES)
+    ]
     col_copies = [
-        send(CS1, CR1.at[d], col_send1.at[d], col_recv1.at[d], 2 + d) for d in range(2)
+        send(CS1.at[d], CR1.at[d], col_send1.at[d], col_recv1.at[d], 2 + d) for d in range(2)
     ]
 
     loads[4].wait()
@@ -250,26 +248,33 @@
         CORR[g] = HC[g] * edge
         VC[g] = HC[g] * jnp.where(slot == 1, turn(edge, 1), turn(edge, -1))
 
+    for copy in col_copies:
+        copy.wait_recv()
+    for g in range(2):
+        from_left, from_right = CR1[0, g], CR1[1, g]
+        base = jnp.where(slot < 2, from_right, from_left)
+        hx = jnp.where(
+            slot == 1, turn(from_right, -1), jnp.where(slot == 2, turn(from_left, 1), 0.0)
+        )
+        edge = jnp.where(walled, 0.0, base + hx * OWN[g])
+        HX[g] = hx
+        EDGE[g] = edge
+        col_effects(g, edge)
+
     chain = (zero, zero)
     for n in range(PIECES):
         for copy in row_copies[n]:
             copy.wait_recv()
-        for half, k0 in spans(n):
-            levels = pl.ds(k0, DEPTH)
-            u_below = RR1[0, n, half, 1] - RR1[0, n, half, 2] * read_rows(PR, BASE, k0, DEPTH)
-            u_above = RR1[1, n, half, 1] + RR1[1, n, half, 2] * read_rows(PR, top, k0, DEPTH)
+        for half, k0 in spans(n, depth):
+            levels = pl.ds(k0, depth)
+            h_below, h_above = RR1[0, n, half, 2], RR1[1, n, half, 2]
+            u_below = RR1[0, n, half, 1] - h_below * read_rows(PR, BASE, k0, depth)
+            u_above = RR1[1, n, half, 1] + h_above * read_rows(PR, top, k0, depth)
             UH[0, levels] = u_below
             UH[1, levels] = u_above
-            row_effects(k0, DEPTH, RR1[0, n, half, 0], RR1[1, n, half, 0], u_below, u_above)
-        if n == 0:
-            for copy in col_copies:
-                copy.wait_recv()
-            for g in range(2):
-                base = jnp.where(slot < 2, CR1[1, 0, g], CR1[0, 0, g])
-                hx = jnp.where(slot < 2, CR1[1, 1, g], CR1[0, 1, g])
-                edge = jnp.where(walled, 0.0, base + hx * OWN[g])
-                EDGE[g] = edge
-                col_effects(g, edge)
+            HH[0, levels] = h_below
+            HH[1, levels] = h_above
+            row_effects(k0, depth, RR1[0, n, half, 0], RR1[1, n, half, 0], u_below, u_above)
         chain = eliminate((n * STEPS // PIECES, (n + 1) * STEPS // PIECES), chain, SRC, E, G, CORR, Y)
     q_bot, q_top = middle(*chain, G, M)
 
@@ -291,15 +296,27 @@
         0, STEPS, substitute, (q_bot, q_top, zero, zero)
     )
 
-    RS2[0, 0] = read_rows(PR, top - 1)
-    RS2[0, 1] = read_rows(PR, top)
-    RS2[1, 0] = read_rows(PR, BASE + 1)
-    RS2[1, 1] = read_rows(PR, BASE)
-    second = [send(RS2.at[d], RR2.at[d], send2.at[d], recv2.at[d], d) for d in range(2)]
-    for g, pack in enumerate((pack_top, pack_bot)):
-        OWN[g] = pack
-        CS2[g] = jnp.where(slot < 2, turn(pack, -2), turn(pack, 2))
-    second += [send(CS2, CR2.at[d], send2.at[2 + d], recv2.at[2 + d], 2 + d) for d in range(2)]
+    depth2 = HALF // PIECES2
+    row_copies2 = []
+    for n in range(PIECES2):
+        for half, k0 in spans(n, depth2):
+            RS2[0, n, half, 0] = read_rows(PR, top - 1, k0, depth2)
+            RS2[0, n, half, 1] = read_rows(PR, top, k0, depth2)
+            RS2[1, n, half, 0] = read_rows(PR, BASE + 1, k0, depth2)
+            RS2[1, n, half, 1] = read_rows(PR, BASE, k0, depth2)
+        row_copies2.append(
+            [
+                send(RS2.at[d, n], RR2.at[d, n], row_send2.at[d, n], row_recv2.at[d, n], d)
+                for d in range(2)
+            ]
+        )
+    OWN[0] = pack_top
+    OWN[1] = pack_bot
+    CS2[0] = jnp.where(slot < 2, pack_bot, turn(pack_top, 2))
+    CS2[1] = jnp.where(slot < 2, turn(pack_top, -2), pack_bot)
+    col_copies2 = [
+        send(CS2.at[d], CR2.at[d], col_send2.at[d], col_recv2.at[d], 2 + d) for d in range(2)
+    ]
 
     nearest = edge_lanes(lane, 1)
 
@@ -310,47 +327,60 @@
                 k = half * HALF + kappa
                 shift = lax.rem(2 * LANES - 4 * kappa - 2, LANES)
                 V[k] = V[k] + jnp.where(nearest, turn(VC[half], shift), 0.0)
-                W[k + 1] = W[k + 1] - S[k] * (PR[k + 1, OWN_ROWS, :] - PR[k, OWN_ROWS, :])
         return carry
 
+    def lift(i, carry):
+        ks, after = pl.ds(i * span, span), pl.ds(i * span + 1, span)
+        W[after] = W[after] - S[ks] * (PR[after, OWN_ROWS, :] - PR[ks, OWN_ROWS, :])
+        return carry
+
     lax.fori_loop(0, STEPS, settle, 0)
+    lax.fori_loop(0, LEVELS // span, lift, 0)
     lax.fori_loop(0, LEVELS // span, inside, 0)
 
-    for copy in second:
+    for copy in col_copies2:
         copy.wait_recv()
-
-    hb, ha = [
-        jnp.concatenate([RR1[d, n, half, 2] for n, half in ORDER], axis=0) for d in range(2)
-    ]
-    u_below = UH[0] - hb * (read_rows(PR, BASE) - RR2[0, 0])
-    u_above = UH[1] + ha * (read_rows(PR, top) - RR2[1, 0])
-    row_effects(0, LEVELS, RR2[0, 1], RR2[1, 1], u_below, u_above)
+    from_left, from_right = CR2[0], CR2[1]
     for g in range(2):
-        hx = jnp.where(slot < 2, CR1[1, 1, g], CR1[0, 1, g])
-        qx = jnp.where(slot < 2, CR2[1, g], CR2[0, g])
-        edge = jnp.where(inner, EDGE[g] + hx * (OWN[g] - qx), qx)
+        if g == 0:
+            qx = jnp.where(slot < 2, from_right, from_left)
+        else:
+            qx = jnp.where(slot < 2, turn(from_right, -2), turn(from_left, 2))
+        edge = jnp.where(inner, EDGE[g] + HX[g] * (OWN[g] - qx), qx)
         col_effects(g, jnp.where(walled, 0.0, edge))
-    for copy in sum(row_copies, col_copies + second):
+    lax.fori_loop(0, STEPS, settle, 0)
+
+    chain = (zero, zero)
+    for n in range(PIECES2):
+        for copy in row_copies2[n]:
+            copy.wait_recv()
+        for half, k0 in spans(n, depth2):
+            levels = pl.ds(k0, depth2)
+            q_below, q_above = RR2[0, n, half, 1], RR2[1, n, half, 1]
+            u_below = UH[0, levels] - HH[0, levels] * (
+                read_rows(PR, BASE, k0, depth2) - RR2[0, n, half, 0]
+            )
+            u_above = UH[1, levels] - HH[1, levels] * (
+                RR2[1, n, half, 0] - read_rows(PR, top, k0, depth2)
+            )
+            row_effects(k0, depth2, q_below, q_above, u_below, u_above)
+        chain = eliminate((n * STEPS // PIECES2, (n + 1) * STEPS // PIECES2), chain, SRC, E, G, CORR, Y)
+    for copy in sum(row_copies + row_copies2, col_copies + col_copies2):
         copy.wait_send()
 
 
-ORDER = [(n, 0) for n in range(PIECES)] + [(n, 1) for n in reversed(range(PIECES))]
-
-
 def finish_kernel(
-    UR, V, W, S, SRC, E, G, M, CORR, VC,
+    UR, V, W, S, Y, G, M,
     u_out, v_out, w_out, p_out,
-    V2, W2, Q, Y, wind_sems, sems,
+    W2, Q, wind_sems, sems,
 ):
     winds = [
         pltpu.make_async_copy(UR.at[:, pl.ds(BASE, ROWS), :], u_out, wind_sems.at[0]),
-        pltpu.make_async_copy(V2, v_out, wind_sems.at[1]),
+        pltpu.make_async_copy(V, v_out, wind_sems.at[1]),
     ]
-    winds[0].start()
-    zero = jnp.zeros(PLANE, F32)
-    y_top, y_bot = eliminate((0, STEPS), (zero, zero), SRC, E, G, CORR, Y, V, VC, V2)
-    winds[1].start()
-    q_bot, q_top = middle(y_top, y_bot, G, M)
+    for copy in winds:
+        copy.start()
+    q_bot, q_top = middle(Y[HALF - 1], Y[HALF], G, M)
 
     def sweep_out(step, carry):
         q_top, q_bot = carry
@@ -399,9 +429,10 @@
     pair = (2,) + PLANE
     vmem = pl.BlockSpec(memory_space=pltpu.VMEM)
     hbm = pl.BlockSpec(memory_space=pltpu.HBM)
-    state = [padded, block, deep, block, block, block, block, PLANE, pair, pair]
-    rows1 = (2, PIECES, 2, 3, DEPTH, LANES)
-    rows2 = (2, 2, LEVELS, LANES)
+    state = [padded, block, deep, block, block, block, PLANE]
+    rows1 = (2, PIECES, 2, 3, HALF // PIECES, LANES)
+    rows2 = (2, PIECES2, 2, 2, HALF // PIECES2, LANES)
+    halo = (2, LEVELS, LANES)
     dma = pltpu.SemaphoreType.DMA
     held = pl.pallas_call(
         exchange_kernel,
@@ -414,15 +445,20 @@
             pltpu.VMEM(block, jnp.bfloat16),
             pltpu.VMEM(block, jnp.bfloat16),
             pltpu.VMEM(block, F32),
+            pltpu.VMEM(block, F32),
+            pltpu.VMEM(pair, F32),
+            pltpu.VMEM(pair, F32),
             pltpu.VMEM(rows1, F32),
             pltpu.VMEM(rows1, F32),
             pltpu.VMEM(rows2, F32),
             pltpu.VMEM(rows2, F32),
-            pltpu.VMEM((2, LEVELS, LANES), F32),
+            pltpu.VMEM(halo, F32),
+            pltpu.VMEM(halo, F32),
             pltpu.VMEM((2,) + pair, F32),
-            pltpu.VMEM((2, 2) + pair, F32),
-            pltpu.VMEM(pair, F32),
             pltpu.VMEM((2,) + pair, F32),
+            pltpu.VMEM(pair, F32),
+            pltpu.VMEM(pair, F32),
+            pltpu.VMEM(pair, F32),
             pltpu.VMEM(pair, F32),
             pltpu.VMEM(pair, F32),
             pltpu.VMEM(pair, F32),
@@ -431,8 +467,10 @@
             dma((2, PIECES)),
             dma((2,)),
             dma((2,)),
-            dma((4,)),
-            dma((4,)),
+            dma((2, PIECES2)),
+            dma((2, PIECES2)),
+            dma((2,)),
+            dma((2,)),
         ],
         compiler_params=pltpu.CompilerParams(
             collective_id=0, has_side_effects=True, vmem_limit_bytes=16 * 1024 * 1024
@@ -446,8 +484,6 @@
         scratch_shapes=[
             pltpu.VMEM(block, F32),
             pltpu.VMEM(block, F32),
-            pltpu.VMEM(block, F32),
-            pltpu.VMEM(block, F32),
             dma((2,)),
             dma((PARTS, 4)),
         ],

time: 33.2 us -> 32.6 us (0.982)
  Pallas kernels: 32.3 us -> 31.8 us
    pallas_call x1, Pallas kernels: 1.85 us -> 1.49 us  [per_device(): pl.pallas_call(finish_kernel, out_shape=[jax.ShapeDtypeStruct(block, F32)...]
where the time goes in v3:
time: 32.6 us; the launch traced here: 32.4 us
  Pallas kernels  31.8 us (98%)
  between operations  0.64 us (2%)
    pallas_call x1, Pallas kernels, per_device(): pl.pallas_call(exchange_kernel, out_shape=[jax.ShapeDtypeStruct(shape, F3...  30.3 us
    pallas_call x1, Pallas kernels, per_device(): pl.pallas_call(finish_kernel, out_shape=[jax.ShapeDtypeStruct(block, F32)...  1.49 us

profile of v3, /device:TPU:6, one launch (start us, length us, event | category | flops | bytes accessed | tf_op | source)
XLA Modules:
  0.0 32.4 jit_solution(500446015279397011)
XLA Ops:
  0.6 30.3 %shard_map.93 = (f32[64,32,128]{2,1,0:T(8,128)S(1)}, f32[64,16,128]{2,1,0:T(8,128)S(1)}, f32[65,16,128]{2,1,0:T(8,128)S(1)}, f32[64,16,128]{2,1,0:T(8,128)S(1)},...) custom-call(f32[64,16,128]{2,1,0:T(8,128)} %u_in.1, f32[64,16,128]{2,1,0:T(8,128)} %v_in.1, ...), custom_call_target="tpu_custom_call" | custom-call | tf_op jit(solution)/shard_map/pallas_call | solution.py:437
  30.9 1.5 %shard_map.94 = (f32[64,16,128]{2,1,0:T(8,128)}, f32[64,16,128]{2,1,0:T(8,128)}, f32[64,16,128]{2,1,0:T(8,128)}, f32[64,16,128]{2,1,0:T(8,128)}) custom-call(f32[64,32,128]{2,1,0:T(8,128)S(1)} %get-tuple-element.11.UR, f32[64,16,128]{2,1,0:T(8,128)S(1)} %get-tuple-element.12.V, f32[65,16,128]{2,1,0:T(8,128)S(1)} %get-tuple-element.13.W, ...), custom_call_target="tpu_custom_call" | custom-call | tf_op jit(solution)/shard_map/pallas_call | solution.py:479

commit v4 on v3

--- a/solution.py
+++ b/solution.py
@@ -14,7 +14,7 @@
 STEPS = HALF // CHUNK
 PIECES = 4
 PIECES2 = 2
-PARTS = 4
+PARTS = 2
 F32 = jnp.float32
 OWN_ROWS = slice(BASE, BASE + ROWS)
 PLANE = (ROWS, LANES)
@@ -70,8 +70,8 @@
 
 def exchange_kernel(
     u_in, v_in, w_in, p_in, c_in, s_in,
-    UR, V, W, S, Y, G, M,
-    PR, H, C16, S16, SRC, E, CORR, VC, RS1, RR1, RS2, RR2, UH, HH,
+    UR, V, W, S, Y, G, M, VC,
+    PR, H, C16, S16, SRC, E, CORR, RS1, RR1, RS2, RR2, UH, HH,
     CS1, CR1, CS2, CR2, OWN, HC, HX, EDGE,
     in_sems, row_send1, row_recv1, col_send1, col_recv1, row_send2, row_recv2, col_send2, col_recv2,
 ):
@@ -80,6 +80,7 @@
     up, down = lax.rem(row + 1, nrow), lax.rem(row + nrow - 1, nrow)
     right, left = lax.rem(col + 1, ncol), lax.rem(col + ncol - 1, ncol)
     targets = [(up, col), (down, col), (row, right), (row, left)]
+    away = 1 - lax.rem(row, 2)
 
     barrier = pltpu.get_barrier_semaphore()
     for target in targets:
@@ -119,17 +120,22 @@
     loads[1].wait()
     loads[2].wait()
 
-    def send(source, landing, send_sem, recv_sem, direction):
-        copy = pltpu.make_async_remote_copy(
+    def remote(source, landing, send_sem, recv_sem, target):
+        return pltpu.make_async_remote_copy(
             src_ref=source,
             dst_ref=landing,
             send_sem=send_sem,
             recv_sem=recv_sem,
-            device_id=targets[direction],
+            device_id=target,
             device_id_type=MESH,
         )
-        copy.start()
-        return copy
+
+    def row_copy(source, landing, send_sem, recv_sem, d, n):
+        target = (lax.rem(row + nrow + 1 - 2 * d, nrow), col)
+        return remote(source.at[d, n], landing.at[d, n], send_sem.at[d, n], recv_sem.at[d, n], target)
+
+    def col_copy(source, landing, send_sem, recv_sem, d):
+        return remote(source.at[d], landing.at[d], send_sem.at[d], recv_sem.at[d], targets[2 + d])
 
     def spans(n, depth):
         return ((0, n * depth), (1, LEVELS - (n + 1) * depth))
@@ -177,13 +183,15 @@
         )
 
     pl.semaphore_wait(barrier, 4)
-    row_copies = [
-        [send(RS1.at[d, n], RR1.at[d, n], row_send1.at[d, n], row_recv1.at[d, n], d) for d in range(2)]
-        for n in range(PIECES)
-    ]
-    col_copies = [
-        send(CS1.at[d], CR1.at[d], col_send1.at[d], col_recv1.at[d], 2 + d) for d in range(2)
-    ]
+    rows1 = (RS1, RR1, row_send1, row_recv1)
+    row_copies = [[row_copy(*rows1, d, n) for d in range(2)] for n in range(PIECES)]
+    col_copies = [col_copy(CS1, CR1, col_send1, col_recv1, d) for d in range(2)]
+    for n in range(PIECES):
+        row_copy(*rows1, away, n).start()
+    for copy in col_copies:
+        copy.start()
+    for n in range(PIECES):
+        row_copy(*rows1, 1 - away, n).start()
 
     loads[4].wait()
 
@@ -297,26 +305,24 @@
     )
 
     depth2 = HALF // PIECES2
-    row_copies2 = []
+    rows2 = (RS2, RR2, row_send2, row_recv2)
+    row_copies2 = [[row_copy(*rows2, d, n) for d in range(2)] for n in range(PIECES2)]
+    col_copies2 = [col_copy(CS2, CR2, col_send2, col_recv2, d) for d in range(2)]
     for n in range(PIECES2):
         for half, k0 in spans(n, depth2):
             RS2[0, n, half, 0] = read_rows(PR, top - 1, k0, depth2)
             RS2[0, n, half, 1] = read_rows(PR, top, k0, depth2)
             RS2[1, n, half, 0] = read_rows(PR, BASE + 1, k0, depth2)
             RS2[1, n, half, 1] = read_rows(PR, BASE, k0, depth2)
-        row_copies2.append(
-            [
-                send(RS2.at[d, n], RR2.at[d, n], row_send2.at[d, n], row_recv2.at[d, n], d)
-                for d in range(2)
-            ]
-        )
+        row_copy(*rows2, away, n).start()
     OWN[0] = pack_top
     OWN[1] = pack_bot
     CS2[0] = jnp.where(slot < 2, pack_bot, turn(pack_top, 2))
     CS2[1] = jnp.where(slot < 2, turn(pack_top, -2), pack_bot)
-    col_copies2 = [
-        send(CS2.at[d], CR2.at[d], col_send2.at[d], col_recv2.at[d], 2 + d) for d in range(2)
-    ]
+    for copy in col_copies2:
+        copy.start()
+    for n in range(PIECES2):
+        row_copy(*rows2, 1 - away, n).start()
 
     nearest = edge_lanes(lane, 1)
 
@@ -348,7 +354,6 @@
             qx = jnp.where(slot < 2, turn(from_right, -2), turn(from_left, 2))
         edge = jnp.where(inner, EDGE[g] + HX[g] * (OWN[g] - qx), qx)
         col_effects(g, jnp.where(walled, 0.0, edge))
-    lax.fori_loop(0, STEPS, settle, 0)
 
     chain = (zero, zero)
     for n in range(PIECES2):
@@ -370,17 +375,18 @@
 
 
 def finish_kernel(
-    UR, V, W, S, Y, G, M,
+    UR, V, W, S, Y, G, M, VC,
     u_out, v_out, w_out, p_out,
-    W2, Q, wind_sems, sems,
+    V2, W2, Q, wind_sem, sems,
 ):
-    winds = [
-        pltpu.make_async_copy(UR.at[:, pl.ds(BASE, ROWS), :], u_out, wind_sems.at[0]),
-        pltpu.make_async_copy(V, v_out, wind_sems.at[1]),
-    ]
-    for copy in winds:
-        copy.start()
+    wind = pltpu.make_async_copy(UR.at[:, pl.ds(BASE, ROWS), :], u_out, wind_sem)
+    wind.start()
     q_bot, q_top = middle(Y[HALF - 1], Y[HALF], G, M)
+    nearest = edge_lanes(lax.broadcasted_iota(jnp.int32, PLANE, 1), 1)
+
+    def settled(k, half):
+        shift = lax.rem(2 * LANES - 4 * (k - half * HALF) - 2, LANES)
+        return V[k] + jnp.where(nearest, turn(VC[half], shift), 0.0)
 
     def sweep_out(step, carry):
         q_top, q_bot = carry
@@ -390,11 +396,13 @@
             q_top = Y[k] + G[k] * q_next
             Q[k] = q_top
             W2[k] = W[k + 1] - S[k] * (q_next - q_top)
+            V2[k] = settled(k, 0)
             k = HALF + step * CHUNK + j
             q_before = q_bot
             q_bot = Y[k] + G[k] * q_before
             Q[k] = q_bot
             W2[k - 1] = W[k] - S[k - 1] * (q_bot - q_before)
+            V2[k] = settled(k, 1)
         return q_top, q_bot
 
     carry = q_bot, q_top
@@ -412,13 +420,15 @@
             (Q, p_out, high, high + part),
             (W2, w_out, low, low + part),
             (W2, w_out, start, stop),
+            (V2, v_out, low, low + part),
+            (V2, v_out, high, high + part),
         )
         for m, (source, target, begin, end) in enumerate(pieces):
             ks = pl.ds(begin, end - begin)
             copy = pltpu.make_async_copy(source.at[ks], target.at[ks], sems.at[n, m])
             copy.start()
             copies.append(copy)
-    for copy in winds + copies:
+    for copy in [wind] + copies:
         copy.wait()
 
 
@@ -429,7 +439,7 @@
     pair = (2,) + PLANE
     vmem = pl.BlockSpec(memory_space=pltpu.VMEM)
     hbm = pl.BlockSpec(memory_space=pltpu.HBM)
-    state = [padded, block, deep, block, block, block, PLANE]
+    state = [padded, block, deep, block, block, block, PLANE, pair]
     rows1 = (2, PIECES, 2, 3, HALF // PIECES, LANES)
     rows2 = (2, PIECES2, 2, 2, HALF // PIECES2, LANES)
     halo = (2, LEVELS, LANES)
@@ -446,7 +456,6 @@
             pltpu.VMEM(block, jnp.bfloat16),
             pltpu.VMEM(block, F32),
             pltpu.VMEM(block, F32),
-            pltpu.VMEM(pair, F32),
             pltpu.VMEM(pair, F32),
             pltpu.VMEM(rows1, F32),
             pltpu.VMEM(rows1, F32),
@@ -484,8 +493,9 @@
         scratch_shapes=[
             pltpu.VMEM(block, F32),
             pltpu.VMEM(block, F32),
-            dma((2,)),
-            dma((PARTS, 4)),
+            pltpu.VMEM(block, F32),
+            dma,
+            dma((PARTS, 6)),
         ],
         compiler_params=pltpu.CompilerParams(vmem_limit_bytes=16 * 1024 * 1024),
     )(*held)

time: 32.6 us -> 32.6 us (level)
  no operation moved by 1% of the time
where the time goes in v4:
time: 32.6 us; the launch traced here: 32.5 us
  Pallas kernels  31.8 us (98%)
  between operations  0.64 us (2%)
    pallas_call x1, Pallas kernels, per_device(): pl.pallas_call(exchange_kernel, out_shape=[jax.ShapeDtypeStruct(shape, F3...  30.3 us
    pallas_call x1, Pallas kernels, per_device(): pl.pallas_call(finish_kernel, out_shape=[jax.ShapeDtypeStruct(block, F32)...  1.52 us

profile of v4, /device:TPU:6, one launch (start us, length us, event | category | flops | bytes accessed | tf_op | source)
XLA Modules:
  0.0 32.5 jit_solution(13184324615133634216)
XLA Ops:
  0.6 30.3 %shard_map.93 = (f32[64,32,128]{2,1,0:T(8,128)S(1)}, f32[64,16,128]{2,1,0:T(8,128)S(1)}, f32[65,16,128]{2,1,0:T(8,128)S(1)}, f32[64,16,128]{2,1,0:T(8,128)S(1)},...) custom-call(f32[64,16,128]{2,1,0:T(8,128)} %u_in.1, ...), custom_call_target="tpu_custom_call" | custom-call | tf_op jit(solution)/shard_map/pallas_call | solution.py:447
  30.9 1.5 %shard_map.94 = (f32[64,16,128]{2,1,0:T(8,128)}, f32[64,16,128]{2,1,0:T(8,128)}, f32[64,16,128]{2,1,0:T(8,128)}, f32[64,16,128]{2,1,0:T(8,128)}) custom-call(f32[64,32,128]{2,1,0:T(8,128)S(1)} %get-tuple-element.12.UR, f32[64,16,128]{2,1,0:T(8,128)S(1)} %get-tuple-element.13.V, f32[65,16,128]{2,1,0:T(8,128)S(1)} %get-tuple-element.14.W, ...), custom_call_target="tpu_custom_call" | custom-call | tf_op jit(solution)/shard_map/pallas_call | solution.py:488

commit v5 on v4

--- a/solution.py
+++ b/solution.py
@@ -308,13 +308,15 @@
     rows2 = (RS2, RR2, row_send2, row_recv2)
     row_copies2 = [[row_copy(*rows2, d, n) for d in range(2)] for n in range(PIECES2)]
     col_copies2 = [col_copy(CS2, CR2, col_send2, col_recv2, d) for d in range(2)]
+
+    def give_rows(d, n):
+        for half, k0 in spans(n, depth2):
+            RS2[d, n, half, 0] = read_rows(PR, top - 1 - d * (ROWS - 3), k0, depth2)
+            RS2[d, n, half, 1] = read_rows(PR, top - d * (ROWS - 1), k0, depth2)
+        row_copy(*rows2, d, n).start()
+
     for n in range(PIECES2):
-        for half, k0 in spans(n, depth2):
-            RS2[0, n, half, 0] = read_rows(PR, top - 1, k0, depth2)
-            RS2[0, n, half, 1] = read_rows(PR, top, k0, depth2)
-            RS2[1, n, half, 0] = read_rows(PR, BASE + 1, k0, depth2)
-            RS2[1, n, half, 1] = read_rows(PR, BASE, k0, depth2)
-        row_copy(*rows2, away, n).start()
+        give_rows(away, n)
     OWN[0] = pack_top
     OWN[1] = pack_bot
     CS2[0] = jnp.where(slot < 2, pack_bot, turn(pack_top, 2))
@@ -322,7 +324,7 @@
     for copy in col_copies2:
         copy.start()
     for n in range(PIECES2):
-        row_copy(*rows2, 1 - away, n).start()
+        give_rows(1 - away, n)
 
     nearest = edge_lanes(lane, 1)
 

time: 32.6 us -> 32.6 us (level)
  no operation moved by 1% of the time
where the time goes in v5:
time: 32.6 us; the launch traced here: 32.4 us
  Pallas kernels  31.8 us (98%)
  between operations  0.64 us (2%)
    pallas_call x1, Pallas kernels, per_device(): pl.pallas_call(exchange_kernel, out_shape=[jax.ShapeDtypeStruct(shape, F3...  30.3 us
    pallas_call x1, Pallas kernels, per_device(): pl.pallas_call(finish_kernel, out_shape=[jax.ShapeDtypeStruct(block, F32)...  1.52 us

profile of v5, /device:TPU:6, one launch (start us, length us, event | category | flops | bytes accessed | tf_op | source)
XLA Modules:
  0.0 32.4 jit_solution(5693976691433956940)
XLA Ops:
  0.6 30.3 %shard_map.93 = (f32[64,32,128]{2,1,0:T(8,128)S(1)}, f32[64,16,128]{2,1,0:T(8,128)S(1)}, f32[65,16,128]{2,1,0:T(8,128)S(1)}, f32[64,16,128]{2,1,0:T(8,128)S(1)},...) custom-call(f32[64,16,128]{2,1,0:T(8,128)} %u_in.1, ...), custom_call_target="tpu_custom_call" | custom-call | tf_op jit(solution)/shard_map/pallas_call | solution.py:449
  30.9 1.5 %shard_map.94 = (f32[64,16,128]{2,1,0:T(8,128)}, f32[64,16,128]{2,1,0:T(8,128)}, f32[64,16,128]{2,1,0:T(8,128)}, f32[64,16,128]{2,1,0:T(8,128)}) custom-call(f32[64,32,128]{2,1,0:T(8,128)S(1)} %get-tuple-element.12.UR, f32[64,16,128]{2,1,0:T(8,128)S(1)} %get-tuple-element.13.V, f32[65,16,128]{2,1,0:T(8,128)S(1)} %get-tuple-element.14.W, ...), custom_call_target="tpu_custom_call" | custom-call | tf_op jit(solution)/shard_map/pallas_call | solution.py:490
